TPU v7x, 256 devices: a whole 4x4x8 slice. The times are simulated.
256 devices in a mesh: pp: 8 (over z), ep: 32 (over x, y, core).
Axes of the slice: x: 4, y: 4, z: 8, core: 2. Of those that a mesh axis runs over, the one named last changes fastest.
Arguments:
- fwd_input: bfloat16 [8, 2048, 3584], P('pp', 'ep'), may hold values from -6 to 6
- fwd_experts: int32 [8, 2048, 2], P('pp', 'ep'), may hold values from 0 to 15, all different within a row; in each aligned block of 64 rows (0 to 63, 64 to 127, ..., all dimensions but the last counted through in order) at most 10 rows name the same one
- fwd_gates: float32 [8, 2048, 2], P('pp', 'ep'), may hold values from 0.1 to 1
- bwd_input: bfloat16 [8, 2048, 3584], P('pp', 'ep'), may hold values from -6 to 6
- bwd_cotangent: bfloat16 [8, 2048, 3584], P('pp', 'ep'), may hold values from -6 to 6
- bwd_experts: int32 [8, 2048, 2], P('pp', 'ep'), may hold values from 0 to 15, all different within a row; in each aligned block of 64 rows (0 to 63, 64 to 127, ..., all dimensions but the last counted through in order) at most 10 rows name the same one
- bwd_gates: float32 [8, 2048, 2], P('pp', 'ep'), may hold values from 0.1 to 1
- w_gate: bfloat16 [8, 3584, 16384], P('pp', None, 'ep'), may hold values from -0.09375 to 0.09375
- w_up: bfloat16 [8, 3584, 16384], P('pp', None, 'ep'), may hold values from -0.09375 to 0.09375
- w_down: bfloat16 [8, 16384, 3584], P('pp', 'ep'), may hold values from -0.1875 to 0.1875
Outputs:
- next_input: bfloat16 [8, 2048, 3584], P('pp', 'ep')
- next_cotangent: bfloat16 [8, 2048, 3584], P('pp', 'ep')
Inputs may be any that keep to these rules, and one draw needn't show every extreme that they name: `fwd_experts`: A token's 2 experts differ; within each block of 64 consecutive tokens of a layer no expert is chosen more than 10 times. `bwd_experts`: as for fwd_experts.
All inputs are finite; a program needn't handle non-finite values.
Results may differ from a plain program's by a relative error of at most 0.009.
Values may be sent and summed in bfloat16 or wider, within the bound.
A program may use at most 128 MiB of HBM per device.

v0:
```python
import jax
import jax.numpy as jnp
from jax import lax
from jax.sharding import PartitionSpec as P

GROUP = 2
TOPK = 2


def from_behind(array, axis, by):
    peers = lax.axis_size(axis)
    return lax.ppermute(array, axis, [(i, (i + by) % peers) for i in range(peers)])


def slot_tables(expert_ids, gate_vals, experts, capacity):
    token_count, pick_count = expert_ids.shape
    one_hot = (
        expert_ids[:, :, None] == jnp.arange(experts, dtype=jnp.int32)[None, None, :]
    ).astype(jnp.int32)
    flat_hot = one_hot.reshape(token_count * pick_count, experts)
    earlier = jnp.cumsum(flat_hot, axis=0) - flat_hot
    slot_pos = jnp.sum(earlier * flat_hot, axis=1).reshape(token_count, pick_count)
    target = expert_ids * capacity + slot_pos
    matches = jnp.arange(experts * capacity, dtype=jnp.int32)[:, None, None] == target[None]
    routing = jnp.sum(matches.astype(jnp.float32), axis=2)
    weighted = jnp.sum(jnp.where(matches, gate_vals[None], 0.0), axis=2)
    return (routing, weighted)


def spread(slot_rows, experts, capacity):
    width = slot_rows.shape[-1]
    blocks = slot_rows.reshape(experts, 1, capacity, width)
    return jnp.broadcast_to(blocks, (experts, GROUP, capacity, width)).reshape(
        experts * GROUP, capacity, width
    )


def collect(returned, experts, capacity):
    width = returned.shape[-1]
    blocks = returned.reshape(experts, GROUP, capacity, width).astype(jnp.float32)
    return jnp.sum(blocks, axis=1).reshape(experts * capacity, width)


def body(
    fwd_input,
    fwd_experts,
    fwd_gates,
    bwd_input,
    bwd_cotangent,
    bwd_experts,
    bwd_gates,
    w_gate,
    w_up,
    w_down,
):
    experts = lax.axis_size("ep") // GROUP
    tok_rows = fwd_input.shape[1]
    capacity = 5 * tok_rows * TOPK // (4 * experts)
    gate_mat = w_gate[0]
    up_mat = w_up[0]
    down_mat = w_down[0]
    fwd_rows = fwd_input[0]
    bwd_rows = bwd_input[0]
    cot_rows = bwd_cotangent[0]
    width = fwd_rows.shape[1]
    fwd_route, fwd_weighted = slot_tables(fwd_experts[0], fwd_gates[0], experts, capacity)
    bwd_route, bwd_weighted = slot_tables(bwd_experts[0], bwd_gates[0], experts, capacity)
    fwd_slots = jnp.dot(
        fwd_route.astype(jnp.bfloat16), fwd_rows, preferred_element_type=jnp.float32
    ).astype(jnp.bfloat16)
    bwd_slots = jnp.dot(
        bwd_route.astype(jnp.bfloat16), bwd_rows, preferred_element_type=jnp.float32
    ).astype(jnp.bfloat16)
    scaled_slots = jnp.dot(
        bwd_weighted, cot_rows.astype(jnp.float32), precision=lax.Precision.HIGHEST
    ).astype(jnp.bfloat16)
    fwd_send = spread(fwd_slots, experts, capacity)
    bwd_send = spread(bwd_slots, experts, capacity)
    scaled_send = spread(scaled_slots, experts, capacity)
    received = lax.all_to_all(fwd_send, "ep", split_axis=0, concat_axis=0, tiled=True)
    shape = received.shape
    flat_in = received.reshape(-1, width)
    pre_gate = jnp.dot(flat_in, gate_mat, preferred_element_type=jnp.float32)
    pre_up = jnp.dot(flat_in, up_mat, preferred_element_type=jnp.float32)
    hidden = (jax.nn.silu(pre_gate) * pre_up).astype(jnp.bfloat16)
    partial_value = jnp.dot(hidden, down_mat, preferred_element_type=jnp.float32).astype(
        jnp.bfloat16
    )
    fwd_back = lax.all_to_all(
        partial_value.reshape(shape), "ep", split_axis=0, concat_axis=0, tiled=True
    )
    received = lax.all_to_all(bwd_send, "ep", split_axis=0, concat_axis=0, tiled=True)
    shape = received.shape
    flat_in = received.reshape(-1, width)
    flat_grad = lax.all_to_all(scaled_send, "ep", split_axis=0, concat_axis=0, tiled=True).reshape(
        -1, width
    )
    pre_gate = jnp.dot(flat_in, gate_mat, preferred_element_type=jnp.float32)
    pre_up = jnp.dot(flat_in, up_mat, preferred_element_type=jnp.float32)
    d_hidden = lax.dot_general(
        flat_grad, down_mat, (((1,), (1,)), ((), ())), preferred_element_type=jnp.float32
    )
    sig = jax.nn.sigmoid(pre_gate)
    d_gate = (d_hidden * pre_up * sig * (1.0 + pre_gate * (1.0 - sig))).astype(jnp.bfloat16)
    d_up = (d_hidden * (pre_gate * sig)).astype(jnp.bfloat16)
    d_input = lax.dot_general(
        d_gate, gate_mat, (((1,), (1,)), ((), ())), preferred_element_type=jnp.float32
    )
    d_input = d_input + lax.dot_general(
        d_up, up_mat, (((1,), (1,)), ((), ())), preferred_element_type=jnp.float32
    )
    bwd_back = lax.all_to_all(
        d_input.astype(jnp.bfloat16).reshape(shape), "ep", split_axis=0, concat_axis=0, tiled=True
    )
    fwd_summed = collect(fwd_back, experts, capacity)
    layer_out = fwd_rows.astype(jnp.float32) + lax.dot_general(
        fwd_weighted, fwd_summed, (((0,), (0,)), ((), ())), precision=lax.Precision.HIGHEST
    )
    bwd_summed = collect(bwd_back, experts, capacity)
    layer_grad = cot_rows.astype(jnp.float32) + lax.dot_general(
        bwd_route, bwd_summed, (((0,), (0,)), ((), ())), precision=lax.Precision.HIGHEST
    )
    next_input = from_behind(layer_out.astype(jnp.bfloat16)[None], "pp", 1)
    next_cotangent = from_behind(layer_grad.astype(jnp.bfloat16)[None], "pp", -1)
    return (next_input, next_cotangent)


def solution(mesh):
    in_specs = (
        P("pp", "ep", None),
        P("pp", "ep", None),
        P("pp", "ep", None),
        P("pp", "ep", None),
        P("pp", "ep", None),
        P("pp", "ep", None),
        P("pp", "ep", None),
        P("pp", None, "ep"),
        P("pp", None, "ep"),
        P("pp", "ep", None),
    )
    out_specs = (P("pp", "ep", None), P("pp", "ep", None))
    return jax.shard_map(body, mesh=mesh, in_specs=in_specs, out_specs=out_specs, check_vma=False)
```

profile of v0, /device:TPU:96, one launch (start us, length us, event | category | flops | bytes accessed | tf_op | source)
XLA Modules:
  0.0 303.4 jit_solution(15874284178255544873)
XLA Ops:
  6.3 2.3 broadcast_in_dim.59
  8.6 7.6 %all-to-all-start = ((bf16[32,10,3584]{2,1,0:T(8,128)(2,1)}), bf16[32,10,3584]{2,1,0:T(8,128)(2,1)}, u32[]{:S(2)}, u32[]{:S(2)}) async-start(bf16[32,10,3584]{2,1,0:T(8,128)(2,1)} %bitcast.76), calls=%async_computation | async-start | bytes 7340032 | tf_op jit(solution)/shard_map/all_to_all | solution.py:80
  18.8 44.0 %all-to-all-done = bf16[32,10,3584]{2,1,0:T(8,128)(2,1)} async-done(((bf16[32,10,3584]{2,1,0:T(8,128)(2,1)}), bf16[32,10,3584]{2,1,0:T(8,128)(2,1)}, u32[]{:S(2)}, u32[]{:S(2)}) %all-to-all-start) | async-done | bytes 2293792 | tf_op jit(solution)/shard_map/all_to_all | solution.py:80
  62.7 2.3 broadcast_in_dim.64
  65.1 6.2 %all-to-all-start.2 = ((bf16[32,10,3584]{2,1,0:T(8,128)(2,1)}), bf16[32,10,3584]{2,1,0:T(8,128)(2,1)}, u32[]{:S(2)}, u32[]{:S(2)}) async-start(bf16[32,10,3584]{2,1,0:T(8,128)(2,1)} %bitcast.78), calls=%async_computation.2 | async-start | bytes 7340032 | tf_op jit(solution)/shard_map/all_to_all | solution.py:95
  72.2 45.6 %all-to-all-done.2 = bf16[32,10,3584]{2,1,0:T(8,128)(2,1)} async-done(((bf16[32,10,3584]{2,1,0:T(8,128)(2,1)}), bf16[32,10,3584]{2,1,0:T(8,128)(2,1)}, u32[]{:S(2)}, u32[]{:S(2)}) %all-to-all-start.2) | async-done | bytes 2293792 | tf_op jit(solution)/shard_map/all_to_all | solution.py:95
  117.9 2.3 broadcast_in_dim.66
  120.2 6.2 %all-to-all-start.3 = ((bf16[32,10,3584]{2,1,0:T(8,128)(2,1)}), bf16[32,10,3584]{2,1,0:T(8,128)(2,1)}, u32[]{:S(2)}, u32[]{:S(2)}) async-start(bf16[32,10,3584]{2,1,0:T(8,128)(2,1)} %bitcast.77), calls=%async_computation.3 | async-start | bytes 7340032 | tf_op jit(solution)/shard_map/all_to_all | solution.py:92
  126.4 3.1 %reshape.64 = bf16[320,3584]{1,0:T(8,128)(2,1)S(1)} reshape(bf16[32,10,3584]{2,1,0:T(8,128)(2,1)} %all-to-all-done) | data formatting | bytes 4587520 | tf_op jit(solution)/shard_map/reshape | solution.py:82
  129.6 3.4 %fusion.17 = f32[320,512]{1,0:T(8,128)S(1)} fusion(bf16[320,3584]{1,0:T(8,128)(2,1)S(1)} %reshape.64, bf16[1,3584,512]{2,1,0:T(8,128)(2,1)} %param.17), kind=kOutput, calls=%fused_computation.26 | convolution fusion | flops 1174405120 | bytes 6619136 | tf_op jit(solution)/shard_map/dot_general | solution.py:83
  133.0 7.2 %convolution_convert_fusion = bf16[320,3584]{1,0:T(8,128)(2,1)} fusion(bf16[1,512,3584]{2,1,0:T(8,128)(2,1)} %param.19, bf16[320,3584]{1,0:T(8,128)(2,1)S(1)} %reshape.64, bf16[1,3584,512]{2,1,0:T(8,128)(2,1)} %param.18, f32[320,512]{1,0:T(8,128)S(1)} %fusion.17), kind=kOutput, calls=%fused_computation.4 | convolution fusion | flops 2350940160 | bytes 12582912 | tf_op jit(solution)/shard_map/dot_general | solution.py:86
  140.1 4.4 %reshape.65 = bf16[32,10,3584]{2,1,0:T(8,128)(2,1)} reshape(bf16[320,3584]{1,0:T(8,128)(2,1)} %convolution_convert_fusion) | data formatting | bytes 4587520 | tf_op jit(solution)/shard_map/reshape | solution.py:90
  144.5 3.1 %reshape.69 = bf16[320,3584]{1,0:T(8,128)(2,1)S(1)} reshape(bf16[32,10,3584]{2,1,0:T(8,128)(2,1)} %all-to-all-done.2) | data formatting | bytes 4587520 | tf_op jit(solution)/shard_map/reshape | solution.py:95
  147.6 25.4 %all-to-all-done.3 = bf16[32,10,3584]{2,1,0:T(8,128)(2,1)} async-done(((bf16[32,10,3584]{2,1,0:T(8,128)(2,1)}), bf16[32,10,3584]{2,1,0:T(8,128)(2,1)}, u32[]{:S(2)}, u32[]{:S(2)}) %all-to-all-start.3) | async-done | bytes 2293792 | tf_op jit(solution)/shard_map/all_to_all | solution.py:92
  173.0 6.4 %all-to-all-start.1 = ((bf16[32,10,3584]{2,1,0:T(8,128)(2,1)}), bf16[32,10,3584]{2,1,0:T(8,128)(2,1)}, u32[]{:S(2)}, u32[]{:S(2)}) async-start(bf16[32,10,3584]{2,1,0:T(8,128)(2,1)} %reshape.65), calls=%async_computation.1 | async-start | bytes 7340032 | tf_op jit(solution)/shard_map/all_to_all | solution.py:89
  179.4 4.5 %reshape.71 = bf16[320,3584]{1,0:T(8,128)(2,1)} reshape(bf16[32,10,3584]{2,1,0:T(8,128)(2,1)} %all-to-all-done.3) | data formatting | bytes 4587520 | tf_op jit(solution)/shard_map/reshape | solution.py:94
  183.9 3.6 %fusion.5 = f32[320,512]{1,0:T(8,128)S(1)} fusion(bf16[320,3584]{1,0:T(8,128)(2,1)S(1)} %reshape.69, bf16[1,512,3584]{2,1,0:T(8,128)(2,1)} %param.19), kind=kOutput, calls=%fused_computation.14 | convolution fusion | flops 1174405120 | bytes 6619136 | tf_op jit(solution)/shard_map/dot_general | solution.py:100
  187.8 2.2 fusion.15
  189.9 8.2 %fusion.13 = f32[320,3584]{1,0:T(8,128)} fusion(bf16[1,3584,512]{2,1,0:T(8,128)(2,1)} %param.17, f32[320,512]{1,0:T(8,128)S(1)} %fusion.5, bf16[320,3584]{1,0:T(8,128)(2,1)S(1)} %copy-done.3, bf16[1,3584,512]{2,1,0:T(8,128)(2,1)} %param.18, f32[320,512]{1,0:T(8,128)} %fusion.15), kind=kOutput, calls=%fused_computation.22 | convolution fusion | flops 2350448640 | bytes 15532032 | tf_op jit(solution)/shard_map/dot_general | solution.py:106
  198.1 5.0 %fusion = bf16[320,3584]{1,0:T(8,128)(2,1)S(1)} fusion(f32[320,3584]{1,0:T(8,128)} %fusion.13, bf16[1,3584,512]{2,1,0:T(8,128)(2,1)} %param.18, f32[320,512]{1,0:T(8,128)S(1)} %fusion.5, f32[320,512]{1,0:T(8,128)} %fusion.15), kind=kOutput, calls=%fused_computation.3 | convolution fusion | flops 1177681920 | bytes 11862016 | tf_op jit(solution)/shard_map/dot_general | solution.py:109
  203.1 2.7 reshape.72
  205.8 19.9 %all-to-all-done.1 = bf16[32,10,3584]{2,1,0:T(8,128)(2,1)} async-done(((bf16[32,10,3584]{2,1,0:T(8,128)(2,1)}), bf16[32,10,3584]{2,1,0:T(8,128)(2,1)}, u32[]{:S(2)}, u32[]{:S(2)}) %all-to-all-start.1) | async-done | bytes 2293792 | tf_op jit(solution)/shard_map/all_to_all | solution.py:89
  225.8 6.3 %all-to-all-start.4 = ((bf16[32,10,3584]{2,1,0:T(8,128)(2,1)}), bf16[32,10,3584]{2,1,0:T(8,128)(2,1)}, u32[]{:S(2)}, u32[]{:S(2)}) async-start(bf16[32,10,3584]{2,1,0:T(8,128)(2,1)} %reshape.72), calls=%async_computation.4 | async-start | bytes 7340032 | tf_op jit(solution)/shard_map/all_to_all | solution.py:112
  232.1 5.1 %convert_reduce_fusion.1 = f32[16,10,3584]{2,1,0:T(8,128)} fusion(bf16[32,10,3584]{2,1,0:T(8,128)(2,1)} %all-to-all-done.1), kind=kLoop, calls=%fused_computation.1 | loop fusion | flops 1720320 | bytes 4587520 | tf_op jit(solution)/shard_map/reduce_sum | solution.py:41
  237.2 2.3 reshape.66
  239.5 2.1 fusion.4
  241.6 3.1 %collective-permute-start = (bf16[1,64,3584]{2,1,0:T(8,128)(2,1)}, bf16[1,64,3584]{2,1,0:T(8,128)(2,1)}, u32[]{:S(2)}, u32[]{:S(2)}) collective-permute-start(bf16[1,64,3584]{2,1,0:T(8,128)(2,1)} %fusion.4), channel_id=1, source_target_pairs={{0,32},{32,64},{64,96},{96,128},{128,160},{160,192},{192,224},{224... | collective-permute-start | bytes 1376264 | tf_op jit(solution)/shard_map/ppermute | solution.py:12
  244.7 34.0 %all-to-all-done.4 = bf16[32,10,3584]{2,1,0:T(8,128)(2,1)} async-done(((bf16[32,10,3584]{2,1,0:T(8,128)(2,1)}), bf16[32,10,3584]{2,1,0:T(8,128)(2,1)}, u32[]{:S(2)}, u32[]{:S(2)}) %all-to-all-start.4) | async-done | bytes 2293792 | tf_op jit(solution)/shard_map/all_to_all | solution.py:112
  278.6 5.0 %convert_reduce_fusion = f32[16,10,3584]{2,1,0:T(8,128)} fusion(bf16[32,10,3584]{2,1,0:T(8,128)(2,1)} %all-to-all-done.4), kind=kLoop, calls=%fused_computation | loop fusion | flops 1720320 | bytes 4587520 | tf_op jit(solution)/shard_map/reduce_sum | solution.py:41
  283.7 2.3 reshape.73
  287.5 13.4 %collective-permute-done.1 = bf16[1,64,3584]{2,1,0:T(8,128)(2,1)S(1)} collective-permute-done((bf16[1,64,3584]{2,1,0:T(8,128)(2,1)S(1)}, bf16[1,64,3584]{2,1,0:T(8,128)(2,1)S(1)}, u32[]{:S(2)}, u32[]{:S(2)}) %collective-permute-start.1) | collective-permute-done | bytes 458784 | tf_op jit(solution)/shard_map/ppermute | solution.py:12
  300.8 1.8 copy.50
  (50 shorter events, 11.6 us)
Async XLA Ops:
  0.6 70.7 %copy-start = (bf16[1,64,3584]{2,1,0:T(8,128)(2,1)S(1)}, bf16[1,64,3584]{2,1,0:T(8,128)(2,1)}, u32[]{:S(2)}) copy-start(bf16[1,64,3584]{2,1,0:T(8,128)(2,1)} %param.13) | copy-start | bytes 1376260
  8.6 7.6 %copy-start.8 = (s32[1,64,2]{1,2,0:T(2,128)S(1)}, s32[1,64,2]{1,2,0:T(2,128)}, u32[]{:S(2)}) copy-start(s32[1,64,2]{1,2,0:T(2,128)} %param.15) | copy-start | bytes 1540
  8.6 8.5 %copy-start.9 = (f32[1,64,2]{1,2,0:T(2,128)S(1)}, f32[1,64,2]{1,2,0:T(2,128)}, u32[]{:S(2)}) copy-start(f32[1,64,2]{1,2,0:T(2,128)} %param.16) | copy-start | bytes 1540
  8.6 8.6 %copy-start.5 = (bf16[1,64,3584]{2,1,0:T(8,128)(2,1)S(1)}, bf16[1,64,3584]{2,1,0:T(8,128)(2,1)}, u32[]{:S(2)}) copy-start(bf16[1,64,3584]{2,1,0:T(8,128)(2,1)} %param.14) | copy-start | bytes 1376260
  8.6 54.2 %all-to-all-start = ((bf16[32,10,3584]{2,1,0:T(8,128)(2,1)}), bf16[32,10,3584]{2,1,0:T(8,128)(2,1)}, u32[]{:S(2)}, u32[]{:S(2)}) async-start(bf16[32,10,3584]{2,1,0:T(8,128)(2,1)} %bitcast.76), calls=%async_computation | async-start | bytes 7340032 | tf_op jit(solution)/shard_map/all_to_all | solution.py:80
  65.1 52.8 %all-to-all-start.2 = ((bf16[32,10,3584]{2,1,0:T(8,128)(2,1)}), bf16[32,10,3584]{2,1,0:T(8,128)(2,1)}, u32[]{:S(2)}, u32[]{:S(2)}) async-start(bf16[32,10,3584]{2,1,0:T(8,128)(2,1)} %bitcast.78), calls=%async_computation.2 | async-start | bytes 7340032 | tf_op jit(solution)/shard_map/all_to_all | solution.py:95
  120.2 52.8 %all-to-all-start.3 = ((bf16[32,10,3584]{2,1,0:T(8,128)(2,1)}), bf16[32,10,3584]{2,1,0:T(8,128)(2,1)}, u32[]{:S(2)}, u32[]{:S(2)}) async-start(bf16[32,10,3584]{2,1,0:T(8,128)(2,1)} %bitcast.77), calls=%async_computation.3 | async-start | bytes 7340032 | tf_op jit(solution)/shard_map/all_to_all | solution.py:92
  173.0 52.7 %all-to-all-start.1 = ((bf16[32,10,3584]{2,1,0:T(8,128)(2,1)}), bf16[32,10,3584]{2,1,0:T(8,128)(2,1)}, u32[]{:S(2)}, u32[]{:S(2)}) async-start(bf16[32,10,3584]{2,1,0:T(8,128)(2,1)} %reshape.65), calls=%async_computation.1 | async-start | bytes 7340032 | tf_op jit(solution)/shard_map/all_to_all | solution.py:89
  183.9 3.6 %copy-start.2 = (bf16[320,3584]{1,0:T(8,128)(2,1)S(1)}, bf16[320,3584]{1,0:T(8,128)(2,1)}, u32[]{:S(2)}) copy-start(bf16[320,3584]{1,0:T(8,128)(2,1)} %reshape.71) | copy-start | bytes 6881284
  183.9 3.8 %copy-start.10 = (bf16[1,3584,512]{2,1,0:T(8,128)(2,1)S(1)}, bf16[1,3584,512]{2,1,0:T(8,128)(2,1)}, u32[]{:S(2)}) copy-start(bf16[1,3584,512]{2,1,0:T(8,128)(2,1)} %param.17) | copy-start | bytes 11010052
  187.8 2.2 copy-start.3
  225.8 52.9 %all-to-all-start.4 = ((bf16[32,10,3584]{2,1,0:T(8,128)(2,1)}), bf16[32,10,3584]{2,1,0:T(8,128)(2,1)}, u32[]{:S(2)}, u32[]{:S(2)}) async-start(bf16[32,10,3584]{2,1,0:T(8,128)(2,1)} %reshape.72), calls=%async_computation.4 | async-start | bytes 7340032 | tf_op jit(solution)/shard_map/all_to_all | solution.py:112
  237.2 2.3 copy-start.4
  237.2 2.3 copy-start.7
  241.6 45.9 %collective-permute-start = (bf16[1,64,3584]{2,1,0:T(8,128)(2,1)}, bf16[1,64,3584]{2,1,0:T(8,128)(2,1)}, u32[]{:S(2)}, u32[]{:S(2)}) collective-permute-start(bf16[1,64,3584]{2,1,0:T(8,128)(2,1)} %fusion.4), channel_id=1, source_target_pairs={{0,32},{32,64},{64,96},{96,128},{128,160},{160,192},{192,224},{224... | collective-permute-start | bytes 1376264 | tf_op jit(solution)/shard_map/ppermute | solution.py:12
  283.6 2.3 copy-start.6
  283.6 19.8 %copy-start.1 = (bf16[1,64,3584]{2,1,0:T(8,128)(2,1)S(1)}, bf16[1,64,3584]{2,1,0:T(8,128)(2,1)}, u32[]{:S(2)}) copy-start(bf16[1,64,3584]{2,1,0:T(8,128)(2,1)} %param.13) | copy-start | bytes 1376260
  287.3 13.5 %collective-permute-start.1 = (bf16[1,64,3584]{2,1,0:T(8,128)(2,1)S(1)}, bf16[1,64,3584]{2,1,0:T(8,128)(2,1)S(1)}, u32[]{:S(2)}, u32[]{:S(2)}) collective-permute-start(bf16[1,64,3584]{2,1,0:T(8,128)(2,1)S(1)} %fusion.3), channel_id=1, source_target_pairs={{0,224},{32,0},{64,32},{96,64},{128,96},{160,128},{192,160},{224,1... | collective-permute-start | bytes 1376264 | tf_op jit(solution)/shard_map/ppermute | solution.py:12
where the time goes:
time: 307 us; the launch traced here: 303 us
  waiting for transfers between devices  182 us (59%)
  starting transfers between devices  36 us (12%)
  matrix products  35.9 us (12%)
  local copies, waits for them, and re-layouts  35.1 us (11%)
  other arithmetic  13.2 us (4%)
    all_to_all x1, waiting for transfers between devices, body(): lax.all_to_all(scaled_send, 'ep', split_axis=0, concat_axis=0, tiled=True)  45.6 us
    all_to_all x1, waiting for transfers between devices, body(): lax.all_to_all(fwd_send, 'ep', split_axis=0, concat_axis=0, tiled=True)  44 us
    all_to_all x1, waiting for transfers between devices, body(): lax.all_to_all(d_input.astype(jnp.bfloat16).reshape(shape), 'ep', split_a...  34 us
    all_to_all x1, waiting for transfers between devices, body(): lax.all_to_all(bwd_send, 'ep', split_axis=0, concat_axis=0, tiled=True)  25.4 us
    all_to_all x1, waiting for transfers between devices, body(): lax.all_to_all(partial_value.reshape(shape), 'ep', split_axis=0, concat_a...  19.9 us
    ppermute x2, waiting for transfers between devices, from_behind(): lax.ppermute(array, axis, [(i, (i + by) % peers) for i in range(peers)])  13.4 us
    reduce_sum x2, other arithmetic, collect(): return jnp.sum(blocks, axis=1).reshape(experts * capacity, width)  10.1 us
    dot_general x1, matrix products, body(): lax.dot_general(d_gate, gate_mat, (((1,), (1,)), ((), ())), preferred_ele...  8.2 us
  transfers between devices with their start and end apart: 7, of which 6 were waited for; matrix products, arithmetic and copies ran while one was open for 23% of the time, Pallas kernels for 0%

commit v1 on v0

v1 whole, which is shorter than its diff:
```python
import jax
import jax.numpy as jnp
from jax import lax
from jax.experimental import pallas as pl
from jax.experimental.pallas import tpu as pltpu
from jax.sharding import PartitionSpec as P

MESH = pl.DeviceIdType.MESH
F32 = jnp.float32
BF16 = jnp.bfloat16

D = 3584
UNIT = 512
TOK = 64
CHIPS = 16
SIDE = 4
ROWS = 160
HALF = D // 2
PIECE = 512
PIECES = D // PIECE
WIDE = HALF + PIECE
MSG = CHIPS * 16
BLOCK = 256


def dot(a, b):
    return lax.dot_general(a, b, (((1,), (0,)), ((), ())), preferred_element_type=F32)


def dot_nt(a, b):
    return lax.dot_general(a, b, (((1,), (1,)), ((), ())), preferred_element_type=F32)


def iota(shape, dim):
    return lax.broadcasted_iota(jnp.int32, shape, dim)


def as_hot(mask):
    return jnp.where(mask, 1.0, 0.0).astype(BF16)


def routing(ids):
    expert = iota((CHIPS, TOK), 0)
    first, second = ids[0:1, :] == expert, ids[1:2, :] == expert
    hits = jnp.where(first | second, 1.0, 0.0)
    before = as_hot(iota((TOK, TOK), 0) < iota((TOK, TOK), 1))
    keys = hits * (dot(hits.astype(BF16), before) + 1.0)
    copies = as_hot((iota((TOK, 9 * TOK), 1) & (TOK - 1)) == iota((TOK, 9 * TOK), 0))
    wide = dot(keys.astype(BF16), copies).astype(BF16)
    key = dot(rows_of_expert(BF16), wide)
    slot = (iota((MSG, 9 * TOK), 0) & 15).astype(F32)
    piece = iota((MSG, 9 * TOK), 1) >> 6
    want_main = slot - 8.0 * piece.astype(F32)
    want_rest = slot - 2.0 * (piece - 2).astype(F32)
    main = (want_main >= 0.0) & (want_main < 8.0) & (key == want_main + 1.0)
    rest = (want_rest >= 0.0) & (want_rest < 2.0) & (key == want_rest + 9.0)
    hot = as_hot(main | rest)
    return key[:, :TOK], hot, first, second


def rows_of_expert(dtype):
    row, expert = iota((MSG, CHIPS), 0), iota((MSG, CHIPS), 1)
    return jnp.where((row >> 4) == expert, 1.0, 0.0).astype(dtype)


def slot_gates(key, first, second, gates):
    per = jnp.where(first, gates[0:1, :], 0.0) + jnp.where(second, gates[1:2, :], 0.0)
    spread = lax.dot_general(
        rows_of_expert(F32),
        per,
        (((1,), (0,)), ((), ())),
        precision=lax.Precision.HIGHEST,
        preferred_element_type=F32,
    )
    slot = iota((MSG, TOK), 0)
    main = key == (slot & 7).astype(F32) + 1.0
    rest = key == (slot & 1).astype(F32) + 9.0
    return (
        jnp.sum(jnp.where(main, spread, 0.0), axis=1, keepdims=True),
        jnp.sum(jnp.where(rest, spread, 0.0), axis=1, keepdims=True),
    )


def place(u, v):
    return (((u >> 1) & 15) << 4) + ((u >> 5) << 1) + (u & 1) == v


def kernel(
    fids, fgates, bids, bgates, xf, xb, cb, gate, up, down,
    out_f, out_b,
    half_x, piece_x, send_b, send_f, recv_b, recv_f, ret_b, ret_f, got_b, got_f,
    wg, wu, wd, rows_v, rows_s, act_a, act_b, rest_z, next_x, next_c,
    n_fids, n_fgates, n_bids, hot_m, hot_r,
    in_sem, w_sem, own_sem, wx_send, wx_recv, z_send, z_recv,
    sb_sem, rb_sem, sf_sem, rf_sem, tb_send, tb_recv, tf_send, tf_recv, ready,
):
    z, me = lax.axis_index("pp"), lax.axis_index("ep")
    sections = lax.axis_size("pp")
    chip, core = me // 2, lax.rem(me, 2)
    above, below = lax.rem(z + 1, sections), lax.rem(z + sections - 1, sections)
    sibling = chip * 2 + 1 - core

    def peer(k):
        x = lax.rem(chip // SIDE + k // SIDE, SIDE)
        y = lax.rem(lax.rem(chip, SIDE) + lax.rem(k, SIDE), SIDE)
        return x * SIDE + y

    barrier = pltpu.get_barrier_semaphore()

    def greet(k, carry):
        pl.semaphore_signal(
            barrier, inc=1, device_id=(z, peer(k) * 2 + core), device_id_type=MESH
        )
        return carry

    lax.fori_loop(1, CHIPS, greet, 0)
    for target in ((z, sibling), (above, me), (below, me)):
        pl.semaphore_signal(barrier, inc=1, device_id=target, device_id_type=MESH)

    loads = []
    for i, src in enumerate((xb, cb, xf)):
        own = []
        for h in range(2):
            own.append(
                pltpu.make_async_copy(
                    src.at[:, pl.ds(h * HALF, HALF)],
                    half_x.at[i, pl.ds(h * TOK, TOK)],
                    in_sem.at[i * 9 + h],
                )
            )
        for k in range(PIECES):
            own.append(
                pltpu.make_async_copy(
                    src.at[:, pl.ds(k * PIECE, PIECE)],
                    piece_x.at[i, pl.ds(k * TOK, TOK)],
                    in_sem.at[i * 9 + 2 + k],
                )
            )
        for copy in own:
            copy.start()
        loads.append(own)
    weights = [
        pltpu.make_async_copy(src, dst.at[0], w_sem.at[i])
        for i, (src, dst) in enumerate(((gate, wg), (up, wu), (down, wd)))
    ]

    def message(i, hot, scales):
        main = dot(hot[:, : 2 * TOK], half_x[i])
        rest = dot(hot[:, 2 * TOK :], piece_x[i])
        if scales is not None:
            main, rest = main * scales[0], rest * scales[1]
        return (
            main.astype(BF16).reshape(CHIPS, 16, HALF),
            rest.astype(BF16).reshape(CHIPS, 16, PIECE),
        )

    key_b, hot_b, first_b, second_b = routing(bids[...])
    scales_b = slot_gates(key_b, first_b, second_b, bgates[...])
    for i in range(2):
        for copy in loads[i]:
            copy.wait()
        main, rest = message(i, hot_b, None if i == 0 else scales_b)
        send_b[:, i, :, :HALF] = main
        send_b[:, i, :, HALF:] = rest

    pl.semaphore_wait(barrier, CHIPS - 1 + 3)

    def to_expert(k, src, dst, send_sem, recv_sem):
        q = peer(k)
        return pltpu.make_async_remote_copy(
            src_ref=src.at[q],
            dst_ref=dst.at[chip],
            send_sem=send_sem.at[k],
            recv_sem=recv_sem.at[k],
            device_id=(z, q * 2 + core),
            device_id_type=MESH,
        )

    def expert_b(k):
        return to_expert(k, send_b, recv_b, sb_sem, rb_sem)

    def expert_f(k):
        return to_expert(k, send_f, recv_f, sf_sem, rf_sem)

    def start_b(k, carry):
        expert_b(k).start()
        return carry

    lax.fori_loop(1, CHIPS, start_b, 0)
    own_b = pltpu.make_async_copy(send_b.at[chip], recv_b.at[chip], own_sem.at[0])
    own_b.start()
    exchange = [
        pltpu.make_async_remote_copy(
            src_ref=src,
            dst_ref=dst.at[1],
            send_sem=wx_send.at[i],
            recv_sem=wx_recv.at[i],
            device_id=(z, sibling),
            device_id_type=MESH,
        )
        for i, (src, dst) in enumerate(((gate, wg), (up, wu), (down, wd)))
    ]
    for copy in weights:
        copy.start()
    for copy in exchange:
        copy.start()
    vertical = [
        pltpu.make_async_remote_copy(
            src_ref=src,
            dst_ref=dst,
            send_sem=z_send.at[i],
            recv_sem=z_recv.at[i],
            device_id=(section, me),
            device_id_type=MESH,
        )
        for i, (src, dst, section) in enumerate(
            (
                (xf, next_x, above),
                (fids, n_fids, above),
                (fgates, n_fgates, above),
                (cb, next_c, below),
                (bids, n_bids, below),
            )
        )
    ]
    for copy in vertical:
        copy.start()

    _, hot_f, _, _ = routing(fids[...])
    for copy in loads[2]:
        copy.wait()
    main, rest = message(2, hot_f, None)
    send_f[:, :, :HALF] = main
    send_f[:, :, HALF:] = rest

    def start_f(k, carry):
        expert_b(k).wait_send()
        expert_f(k).start()
        return carry

    lax.fori_loop(1, CHIPS, start_f, 0)
    own_f = pltpu.make_async_copy(send_f.at[chip], recv_f.at[chip], own_sem.at[1])
    own_f.start()

    def flip(hot):
        n = hot.shape[1]
        unit = as_hot(iota((n, n), 0) == iota((n, n), 1))
        return dot_nt(unit, hot).astype(BF16)

    for i in (1, 2, 4):
        vertical[i].wait_recv()
    _, hot, _, _ = routing(n_bids[...])
    hot_m[0] = flip(hot[:, : 2 * TOK])
    hot_r[0] = flip(hot[:, 2 * TOK :])
    key, hot, first, second = routing(n_fids[...])
    scale_m, scale_r = slot_gates(key, first, second, n_fgates[...])
    high_m, high_r = scale_m.astype(BF16).astype(F32), scale_r.astype(BF16).astype(F32)
    hot_main, hot_rest = hot[:, : 2 * TOK].astype(F32), hot[:, 2 * TOK :].astype(F32)
    hot_m[1] = flip((hot_main * high_m).astype(BF16))
    hot_r[1] = flip((hot_rest * high_r).astype(BF16))
    hot_m[2] = flip((hot_main * (scale_m - high_m)).astype(BF16))
    hot_r[2] = flip((hot_rest * (scale_r - high_r)).astype(BF16))

    def unpack(load, dst):
        def step(i, carry):
            pair = load(pl.ds(2 * i, 2), pl.ds(0, HALF)).astype(F32)
            halves = pair.reshape(2, 2, 8, HALF)
            rows = pl.ds(pl.multiple_of(16 * i, 16), 16)
            dst[rows, :HALF] = halves[:, 0].reshape(16, HALF).astype(BF16)
            dst[rows, HALF:] = halves[:, 1].reshape(16, HALF).astype(BF16)
            return carry

        lax.fori_loop(0, CHIPS // 2, step, 0)
        rest = load(pl.ds(0, CHIPS), pl.ds(HALF, PIECE)).reshape(MSG, PIECE)
        n = PIECES * 32
        order = as_hot(place(iota((n, MSG), 0), iota((n, MSG), 1)))
        plain = dot(order, rest).astype(BF16)
        for k in range(PIECES):
            dst[128:ROWS, k * PIECE : (k + 1) * PIECE] = plain[32 * k : 32 * k + 32]

    def pack(column, dst):
        def keep(c, rows):
            rest_z[
                pl.ds(pl.multiple_of((c // 2) * 32, 32), 32),
                pl.ds(pl.multiple_of(lax.rem(c, 2) * BLOCK, BLOCK), BLOCK),
            ] = rows.astype(BF16)

        def step(n, carry):
            low, high = column(n), column(n + 7)
            main = jnp.concatenate(
                [low[:128].reshape(CHIPS, 8, BLOCK), high[:128].reshape(CHIPS, 8, BLOCK)], axis=1
            )
            dst[:, :, pl.ds(pl.multiple_of(n * BLOCK, BLOCK), BLOCK)] = main.astype(BF16)
            keep(n, low[128:])
            keep(n + 7, high[128:])
            return carry

        lax.fori_loop(0, HALF // BLOCK, step, 0)
        n = PIECES * 32
        order = as_hot(place(iota((MSG, n), 1), iota((MSG, n), 0)))
        dst[:, :, HALF:] = dot(order, rest_z[...]).astype(BF16).reshape(CHIPS, 16, PIECE)

    def unit_of(u):
        return u // 2, pl.ds(pl.multiple_of(lax.rem(u, 2) * BLOCK, BLOCK), BLOCK)

    def act_of(u):
        return pl.ds(pl.multiple_of(u * BLOCK, BLOCK), BLOCK)

    def arrive_b(k, carry):
        expert_b(k).wait_recv()
        return carry

    lax.fori_loop(1, CHIPS, arrive_b, 0)
    own_b.wait()
    pl.semaphore_signal(ready.at[0], inc=1, device_id=(above, me), device_id_type=MESH)
    pl.semaphore_signal(ready.at[1], inc=1, device_id=(below, me), device_id_type=MESH)
    unpack(lambda i, j: recv_b[i, 0, :, j], rows_v)
    unpack(lambda i, j: recv_b[i, 1, :, j], rows_s)
    for copy in weights:
        copy.wait()

    def hidden_b(u, carry):
        j, cols = unit_of(u)
        a = dot(rows_v[...], wg[j, :, cols])
        b = dot(rows_v[...], wu[j, :, cols])
        dh = dot_nt(rows_s[...], wd[j, cols, :])
        sig = jax.nn.sigmoid(a)
        act_a[:, act_of(u)] = (dh * b * sig * (1.0 + a * (1.0 - sig))).astype(BF16)
        act_b[:, act_of(u)] = (dh * (a * sig)).astype(BF16)
        return carry

    lax.fori_loop(0, 2, hidden_b, 0)
    for copy in exchange:
        copy.wait_recv()
    lax.fori_loop(2, 4, hidden_b, 0)

    def column_b(n):
        rows = pl.ds(pl.multiple_of(n * BLOCK, BLOCK), BLOCK)
        total = jnp.zeros((ROWS, BLOCK), F32)
        for j in range(2):
            total += dot_nt(act_a[:, j * UNIT : (j + 1) * UNIT], wg[j, rows, :])
            total += dot_nt(act_b[:, j * UNIT : (j + 1) * UNIT], wu[j, rows, :])
        return total

    pack(column_b, ret_b)

    def to_token(k, section, src, dst, send_sem, recv_sem):
        q = peer(k)
        return pltpu.make_async_remote_copy(
            src_ref=src.at[q],
            dst_ref=dst.at[chip],
            send_sem=send_sem.at[k],
            recv_sem=recv_sem.at[k],
            device_id=(section, q * 2 + core),
            device_id_type=MESH,
        )

    def token_b(k):
        return to_token(k, below, ret_b, got_b, tb_send, tb_recv)

    def token_f(k):
        return to_token(k, above, ret_f, got_f, tf_send, tf_recv)

    pl.semaphore_wait(ready.at[0], 1)

    def return_b(k, carry):
        token_b(k).start()
        return carry

    lax.fori_loop(0, CHIPS, return_b, 0)

    def arrive_f(k, carry):
        expert_f(k).wait_recv()
        return carry

    lax.fori_loop(1, CHIPS, arrive_f, 0)
    own_f.wait()
    unpack(lambda i, j: recv_f[i, :, j], rows_v)

    def hidden_f(u, carry):
        j, cols = unit_of(u)
        a = dot(rows_v[...], wg[j, :, cols])
        b = dot(rows_v[...], wu[j, :, cols])
        act_a[:, act_of(u)] = (a * jax.nn.sigmoid(a) * b).astype(BF16)
        return carry

    lax.fori_loop(0, 4, hidden_f, 0)

    def column_f(n):
        cols = pl.ds(pl.multiple_of(n * BLOCK, BLOCK), BLOCK)
        total = jnp.zeros((ROWS, BLOCK), F32)
        for j in range(2):
            total += dot(act_a[:, j * UNIT : (j + 1) * UNIT], wd[j, :, cols])
        return total

    pack(column_f, ret_f)
    pl.semaphore_wait(ready.at[1], 1)

    def return_f(k, carry):
        token_f(k).start()
        return carry

    lax.fori_loop(0, CHIPS, return_f, 0)

    def combine(got, kinds, base, out):
        main = sum(dot(hot_m[i], got[:, :, :HALF].reshape(MSG, HALF)) for i in kinds)
        rest = sum(dot(hot_r[i], got[:, :, HALF:].reshape(MSG, PIECE)) for i in kinds)
        for c in range(2 * HALF // BLOCK):
            h, at = c // 7, (c % 7) * BLOCK
            k, off = c // 2, (c % 2) * BLOCK
            cols = slice(c * BLOCK, (c + 1) * BLOCK)
            out[:, cols] = (
                base[:, cols].astype(F32)
                + main[h * TOK : (h + 1) * TOK, at : at + BLOCK]
                + rest[k * TOK : (k + 1) * TOK, off : off + BLOCK]
            ).astype(BF16)

    for i in (0, 3):
        vertical[i].wait_recv()

    def back_b(k, carry):
        token_b(k).wait_recv()
        return carry

    def back_f(k, carry):
        token_f(k).wait_recv()
        return carry

    lax.fori_loop(0, CHIPS, back_b, 0)
    combine(got_b, (0,), next_c, out_b)
    lax.fori_loop(0, CHIPS, back_f, 0)
    combine(got_f, (1, 2), next_x, out_f)

    def sent(k, carry):
        token_b(k).wait_send()
        token_f(k).wait_send()
        return carry

    def sent_f(k, carry):
        expert_f(k).wait_send()
        return carry

    lax.fori_loop(1, CHIPS, sent_f, 0)
    lax.fori_loop(0, CHIPS, sent, 0)
    for copy in exchange + vertical:
        copy.wait_send()


def body(
    fwd_input, fwd_experts, fwd_gates, bwd_input, bwd_cotangent, bwd_experts, bwd_gates,
    w_gate, w_up, w_down,
):
    vmem, anywhere = pl.BlockSpec(memory_space=pltpu.VMEM), pl.BlockSpec(memory_space=pl.ANY)
    token_rows = jax.ShapeDtypeStruct((TOK, D), BF16)
    messages = pltpu.VMEM((CHIPS, 16, WIDE), BF16)
    pairs = pltpu.VMEM((CHIPS, 2, 16, WIDE), BF16)
    sixteen = pltpu.SemaphoreType.DMA((CHIPS,))
    out_f, out_b = pl.pallas_call(
        kernel,
        out_shape=(token_rows, token_rows),
        in_specs=[vmem] * 4 + [anywhere] * 6,
        out_specs=(vmem, vmem),
        scratch_shapes=[
            pltpu.VMEM((3, 2 * TOK, HALF), BF16),
            pltpu.VMEM((3, PIECES * TOK, PIECE), BF16),
            pairs, messages, pairs, messages, messages, messages, messages, messages,
            pltpu.VMEM((2, D, UNIT), BF16),
            pltpu.VMEM((2, D, UNIT), BF16),
            pltpu.VMEM((2, UNIT, D), BF16),
            pltpu.VMEM((ROWS, D), BF16),
            pltpu.VMEM((ROWS, D), BF16),
            pltpu.VMEM((ROWS, 2 * UNIT), BF16),
            pltpu.VMEM((ROWS, 2 * UNIT), BF16),
            pltpu.VMEM((PIECES * 32, PIECE), BF16),
            pltpu.VMEM((TOK, D), BF16),
            pltpu.VMEM((TOK, D), BF16),
            pltpu.VMEM((2, TOK), jnp.int32),
            pltpu.VMEM((2, TOK), F32),
            pltpu.VMEM((2, TOK), jnp.int32),
            pltpu.VMEM((3, 2 * TOK, MSG), BF16),
            pltpu.VMEM((3, PIECES * TOK, MSG), BF16),
            pltpu.SemaphoreType.DMA((27,)),
            pltpu.SemaphoreType.DMA((3,)),
            pltpu.SemaphoreType.DMA((2,)),
            pltpu.SemaphoreType.DMA((3,)),
            pltpu.SemaphoreType.DMA((3,)),
            pltpu.SemaphoreType.DMA((5,)),
            pltpu.SemaphoreType.DMA((5,)),
            sixteen, sixteen, sixteen, sixteen, sixteen, sixteen, sixteen, sixteen,
            pltpu.SemaphoreType.REGULAR((2,)),
        ],
        compiler_params=pltpu.CompilerParams(
            collective_id=0, has_side_effects=True, vmem_limit_bytes=60 << 20
        ),
        name="relay_experts",
    )(
        fwd_experts[0].T, fwd_gates[0].T, bwd_experts[0].T, bwd_gates[0].T,
        fwd_input[0], bwd_input[0], bwd_cotangent[0], w_gate[0], w_up[0], w_down[0],
    )
    return out_f[None], out_b[None]


def solution(mesh):
    tokens = P("pp", "ep", None)
    in_specs = (tokens,) * 7 + (P("pp", None, "ep"), P("pp", None, "ep"), tokens)
    return jax.shard_map(
        body, mesh=mesh, in_specs=in_specs, out_specs=(tokens, tokens), check_vma=False
    )
```

time: 307 us -> 108 us (0.35)
  the two profiles are of different devices: /device:TPU:96 before, /device:TPU:2 now
where the time goes in v1:
time: 108 us
  Pallas kernels  104 us (96%)
  local copies, waits for them, and re-layouts  3.63 us (3%)
    pallas_call x1, Pallas kernels, body(): pl.pallas_call(kernel, out_shape=(token_rows, token_rows), in_specs=[vmem...  104 us
    unnamed x2, local copies, waits for them, and re-layouts  3.63 us

profile of v1, /device:TPU:2, one launch (start us, length us, event | category | flops | bytes accessed | tf_op | source)
XLA Modules:
  0.0 108.0 jit_solution(15937076373217183556)
XLA Ops:
  0.6 103.7 %relay_experts.1 = (bf16[64,3584]{1,0:T(8,128)(2,1)}, bf16[64,3584]{1,0:T(8,128)(2,1)}) custom-call(s32[2,64]{1,0:T(2,128)} %bitcast.28, f32[2,64]{1,0:T(2,128)} %bitcast.29, s32[2,64]{1,0:T(2,128)} %bitcast.30, f32[2,64]{1,0:T(2,128)} %bitcast.31, bf16[64,3584]{1,0:T(8,128)(2,1)} %bitcast.25, bf16[64,3584]{1,0:T(8,128)(2,1)} %bitcast.26, ...), custom_call_target="tpu_custom_call" | custom-call | tf_op jit(solution)/shard_map/relay_experts/pallas_call | solution.py:458
  104.4 1.8 %copy.14 = bf16[1,64,3584]{2,1,0:T(8,128)(2,1)} copy(bf16[1,64,3584]{2,1,0:T(8,128)(2,1)} %bitcast.24) | data formatting | bytes 917504
  106.2 1.8 %copy.15 = bf16[1,64,3584]{2,1,0:T(8,128)(2,1)} copy(bf16[1,64,3584]{2,1,0:T(8,128)(2,1)} %bitcast.23) | data formatting | bytes 917504

commit v2 on v1

v2 whole, which is shorter than its diff:
```python
import jax
import jax.numpy as jnp
from jax import lax
from jax.experimental import pallas as pl
from jax.experimental.pallas import tpu as pltpu
from jax.sharding import PartitionSpec as P

MESH = pl.DeviceIdType.MESH
F32 = jnp.float32
BF16 = jnp.bfloat16

D = 3584
UNIT = 512
TOK = 64
CHIPS = 16
SIDE = 4
ROWS = 160
HALF = D // 2
PIECE = 512
PIECES = D // PIECE
WIDE = HALF + PIECE
MSG = CHIPS * 16
BLOCK = 256
LANES = 128
CHUNKS = 4
CHUNK = 2 * BLOCK + LANES
HOTS = 10 * TOK
FAR_FIRST = (10, 9, 14, 11, 6, 5, 13, 15, 7, 8, 2, 4, 1, 12, 3)


def dot(a, b):
    return lax.dot_general(a, b, (((1,), (0,)), ((), ())), preferred_element_type=F32)


def dot_nt(a, b):
    return lax.dot_general(a, b, (((1,), (1,)), ((), ())), preferred_element_type=F32)


def iota(shape, dim):
    return lax.broadcasted_iota(jnp.int32, shape, dim)


def as_hot(mask):
    return jnp.where(mask, 1.0, 0.0).astype(BF16)


def routing(ids):
    expert = iota((CHIPS, TOK), 0)
    first, second = ids[0:1, :] == expert, ids[1:2, :] == expert
    hits = jnp.where(first | second, 1.0, 0.0)
    before = as_hot(iota((TOK, TOK), 0) < iota((TOK, TOK), 1))
    keys = hits * (dot(hits.astype(BF16), before) + 1.0)
    copies = as_hot((iota((TOK, HOTS), 1) & (TOK - 1)) == iota((TOK, HOTS), 0))
    wide = dot(keys.astype(BF16), copies).astype(BF16)
    key = dot(rows_of_expert(BF16), wide)
    slot = (iota((MSG, HOTS), 0) & 15).astype(F32)
    piece = iota((MSG, HOTS), 1) >> 6
    want_main = slot - 8.0 * piece.astype(F32)
    want_rest = slot - 2.0 * (piece - 2).astype(F32)
    main = (want_main >= 0.0) & (want_main < 8.0) & (key == want_main + 1.0)
    rest = (want_rest >= 0.0) & (want_rest < 2.0) & (key == want_rest + 9.0)
    hot = as_hot(main | rest)
    return key[:, :TOK], hot, first, second


def rows_of_expert(dtype):
    row, expert = iota((MSG, CHIPS), 0), iota((MSG, CHIPS), 1)
    return jnp.where((row >> 4) == expert, 1.0, 0.0).astype(dtype)


def slot_gates(key, first, second, gates):
    per = jnp.where(first, gates[0:1, :], 0.0) + jnp.where(second, gates[1:2, :], 0.0)
    spread = lax.dot_general(
        rows_of_expert(F32),
        per,
        (((1,), (0,)), ((), ())),
        precision=lax.Precision.HIGHEST,
        preferred_element_type=F32,
    )
    slot = iota((MSG, TOK), 0)
    main = key == (slot & 7).astype(F32) + 1.0
    rest = key == (slot & 1).astype(F32) + 9.0
    return (
        jnp.sum(jnp.where(main, spread, 0.0), axis=1, keepdims=True),
        jnp.sum(jnp.where(rest, spread, 0.0), axis=1, keepdims=True),
    )


def place(u, v):
    return (((u >> 1) & 15) << 4) + ((u >> 5) << 1) + (u & 1) == v


def kernel(
    fids, fgates, bids, bgates, xf, xb, cb, gate, up, down,
    out_f, out_b,
    half_x, piece_x, send_v, send_s, send_f, recv_v, recv_s, recv_f, ret_b, ret_f, got_b, got_f,
    wg, wu, wd, rows_v, rows_s, act_a, act_b, base_x, base_c, sum_f, sum_b, hot_m, hot_r,
    in_sem, base_sem, w_sem, own_sem, wx_send, wx_recv,
    sv_sem, rv_sem, ss_sem, rs_sem, sf_sem, rf_sem,
    tb_send, tb_recv, tf_send, tf_recv, hb_send, hb_recv, hf_send, hf_recv,
):
    z, me = lax.axis_index("pp"), lax.axis_index("ep")
    sections = lax.axis_size("pp")
    chip, core = me // 2, lax.rem(me, 2)
    above, below = lax.rem(z + 1, sections), lax.rem(z + sections - 1, sections)
    sibling = chip * 2 + 1 - core

    def peer(k):
        x = lax.rem(chip // SIDE + k // SIDE, SIDE)
        y = lax.rem(lax.rem(chip, SIDE) + k % SIDE, SIDE)
        return x * SIDE + y

    barrier = pltpu.get_barrier_semaphore()
    for k in FAR_FIRST:
        pl.semaphore_signal(
            barrier, inc=1, device_id=(z, peer(k) * 2 + core), device_id_type=MESH
        )
    for target in ((z, sibling), (above, me), (below, me)):
        pl.semaphore_signal(barrier, inc=1, device_id=target, device_id_type=MESH)

    loads = []
    for i, src in enumerate((xb, cb, xf)):
        own = []
        for h in range(2):
            own.append(
                pltpu.make_async_copy(
                    src.at[:, pl.ds(h * HALF, HALF)],
                    half_x.at[i, pl.ds(h * TOK, TOK)],
                    in_sem.at[i * 9 + h],
                )
            )
        for k in range(PIECES):
            own.append(
                pltpu.make_async_copy(
                    src.at[:, pl.ds(k * PIECE, PIECE)],
                    piece_x.at[i, pl.ds(k * TOK, TOK)],
                    in_sem.at[i * 9 + 2 + k],
                )
            )
        for copy in own:
            copy.start()
        loads.append(own)
    weights = [
        pltpu.make_async_copy(src, dst.at[0], w_sem.at[i])
        for i, (src, dst) in enumerate(((gate, wg), (up, wu), (down, wd)))
    ]
    bases = [
        pltpu.make_async_copy(xf, base_x, base_sem.at[0]),
        pltpu.make_async_copy(cb, base_c, base_sem.at[1]),
    ]

    def message(i, hot, scales, dst):
        for copy in loads[i]:
            copy.wait()
        main = dot(hot[:, : 2 * TOK], half_x[i])
        rest = dot(hot[:, 2 * TOK : 2 * TOK + PIECES * TOK], piece_x[i])
        if scales is not None:
            main, rest = main * scales[0], rest * scales[1]
        dst[:, :, :HALF] = main.astype(BF16).reshape(CHIPS, 16, HALF)
        dst[:, :, HALF:] = rest.astype(BF16).reshape(CHIPS, 16, PIECE)

    def to_expert(k, src, dst, send_sem, recv_sem):
        q = peer(k)
        return pltpu.make_async_remote_copy(
            src_ref=src.at[q],
            dst_ref=dst.at[chip],
            send_sem=send_sem.at[k],
            recv_sem=recv_sem.at[k],
            device_id=(z, q * 2 + core),
            device_id_type=MESH,
        )

    def expert_v(k):
        return to_expert(k, send_v, recv_v, sv_sem, rv_sem)

    def expert_s(k):
        return to_expert(k, send_s, recv_s, ss_sem, rs_sem)

    def expert_f(k):
        return to_expert(k, send_f, recv_f, sf_sem, rf_sem)

    keep_v, keep_s, keep_f = (
        pltpu.make_async_copy(src.at[chip], dst.at[chip], own_sem.at[i])
        for i, (src, dst) in enumerate(((send_v, recv_v), (send_s, recv_s), (send_f, recv_f)))
    )

    key_b, hot_b, first_b, second_b = routing(bids[...])
    message(0, hot_b, None, send_v)
    pl.semaphore_wait(barrier, CHIPS - 1 + 3)
    for k in FAR_FIRST:
        expert_v(k).start()
    keep_v.start()
    message(1, hot_b, slot_gates(key_b, first_b, second_b, bgates[...]), send_s)
    for k in FAR_FIRST:
        expert_s(k).start()
    keep_s.start()

    exchange = [
        pltpu.make_async_remote_copy(
            src_ref=src,
            dst_ref=dst.at[1],
            send_sem=wx_send.at[i],
            recv_sem=wx_recv.at[i],
            device_id=(z, sibling),
            device_id_type=MESH,
        )
        for i, (src, dst) in enumerate(((gate, wg), (up, wu), (down, wd)))
    ]
    for copy in weights + exchange + bases:
        copy.start()

    key_f, hot_f, first_f, second_f = routing(fids[...])
    message(2, hot_f, None, send_f)
    for k in FAR_FIRST:
        expert_s(k).wait_send()
        expert_f(k).start()
    keep_f.start()

    def flip(hot):
        n = hot.shape[1]
        unit = as_hot(iota((n, n), 0) == iota((n, n), 1))
        return dot_nt(unit, hot).astype(BF16)

    hot_m[0] = flip(hot_b[:, : 2 * TOK])
    hot_r[0] = flip(hot_b[:, 2 * TOK :])
    scale_m, scale_r = slot_gates(key_f, first_f, second_f, fgates[...])
    high_m, high_r = scale_m.astype(BF16).astype(F32), scale_r.astype(BF16).astype(F32)
    hot_main, hot_rest = hot_f[:, : 2 * TOK].astype(F32), hot_f[:, 2 * TOK :].astype(F32)
    hot_m[1] = flip((hot_main * high_m).astype(BF16))
    hot_r[1] = flip((hot_rest * high_r).astype(BF16))
    hot_m[2] = flip((hot_main * (scale_m - high_m)).astype(BF16))
    hot_r[2] = flip((hot_rest * (scale_r - high_r)).astype(BF16))

    def unpack(src, dst):
        def step(i, carry):
            pair = src[pl.ds(2 * i, 2), :, :HALF].astype(F32)
            halves = pair.reshape(2, 2, 8, HALF)
            rows = pl.ds(pl.multiple_of(16 * i, 16), 16)
            dst[rows, :HALF] = halves[:, 0].reshape(16, HALF).astype(BF16)
            dst[rows, HALF:] = halves[:, 1].reshape(16, HALF).astype(BF16)
            return carry

        lax.fori_loop(0, CHIPS // 2, step, 0)
        rest = src[:, :, HALF:].reshape(MSG, PIECE)
        n = PIECES * 32
        order = as_hot(place(iota((n, MSG), 0), iota((n, MSG), 1)))
        plain = dot(order, rest).astype(BF16)
        for k in range(PIECES):
            dst[128:ROWS, k * PIECE : (k + 1) * PIECE] = plain[32 * k : 32 * k + 32]

    def unit_of(u):
        return u // 2, pl.ds(pl.multiple_of(lax.rem(u, 2) * BLOCK, BLOCK), BLOCK)

    def act_of(u):
        return pl.ds(pl.multiple_of(u * BLOCK, BLOCK), BLOCK)

    def to_token(k, c, width, src, dst, send_sem, recv_sem):
        q = peer(k)
        return pltpu.make_async_remote_copy(
            src_ref=src.at[c, q, :, pl.ds(0, width)],
            dst_ref=dst.at[c, chip, :, pl.ds(0, width)],
            send_sem=send_sem.at[c],
            recv_sem=recv_sem.at[c],
            device_id=(z, q * 2 + core),
            device_id_type=MESH,
        )

    def emit(column, c, steps, ret, got, send_sem, recv_sem):
        lows = [column(2 * c + i) for i in range(steps)]
        highs = [column(2 * c + i + 7) for i in range(steps)]
        for i in range(steps):
            main = jnp.concatenate(
                [y[:128].reshape(CHIPS, 8, BLOCK) for y in (lows[i], highs[i])], axis=1
            )
            ret[c, :, :, i * BLOCK : (i + 1) * BLOCK] = main.astype(BF16)
        rests = [
            y[128:, j * LANES : (j + 1) * LANES] for y in lows + highs for j in range(BLOCK // LANES)
        ]
        n = len(rests) * 32
        order = as_hot(place(iota((MSG, n), 1), iota((MSG, n), 0)))
        rest = dot(order, jnp.concatenate(rests, axis=0).astype(BF16))
        wide = steps * BLOCK
        ret[c, :, :, wide : wide + LANES] = rest.astype(BF16).reshape(CHIPS, 16, LANES)
        for k in FAR_FIRST:
            to_token(k, c, wide + LANES, ret, got, send_sem, recv_sem).start()
        pltpu.make_async_copy(
            ret.at[c, chip, :, pl.ds(0, wide + LANES)],
            got.at[c, chip, :, pl.ds(0, wide + LANES)],
            recv_sem.at[c],
        ).start()

    def emit_all(column, ret, got, send_sem, recv_sem):
        def step(c, carry):
            emit(column, c, 2, ret, got, send_sem, recv_sem)
            return carry

        lax.fori_loop(0, CHUNKS - 1, step, 0)
        emit(column, CHUNKS - 1, 1, ret, got, send_sem, recv_sem)

    for k in FAR_FIRST:
        expert_v(k).wait_recv()
    keep_v.wait()
    unpack(recv_v, rows_v)
    for k in FAR_FIRST:
        expert_s(k).wait_recv()
    keep_s.wait()
    unpack(recv_s, rows_s)
    for copy in weights:
        copy.wait()

    def hidden_b(u, carry):
        j, cols = unit_of(u)
        a = dot(rows_v[...], wg[j, :, cols])
        b = dot(rows_v[...], wu[j, :, cols])
        dh = dot_nt(rows_s[...], wd[j, cols, :])
        sig = jax.nn.sigmoid(a)
        act_a[:, act_of(u)] = (dh * b * sig * (1.0 + a * (1.0 - sig))).astype(BF16)
        act_b[:, act_of(u)] = (dh * (a * sig)).astype(BF16)
        return carry

    lax.fori_loop(0, 2, hidden_b, 0)
    for copy in exchange:
        copy.wait_recv()
    lax.fori_loop(2, 4, hidden_b, 0)

    def column_b(n):
        rows = pl.ds(pl.multiple_of(n * BLOCK, BLOCK), BLOCK)
        total = jnp.zeros((ROWS, BLOCK), F32)
        for j in range(2):
            total += dot_nt(act_a[:, j * UNIT : (j + 1) * UNIT], wg[j, rows, :])
            total += dot_nt(act_b[:, j * UNIT : (j + 1) * UNIT], wu[j, rows, :])
        return total

    emit_all(column_b, ret_b, got_b, tb_send, tb_recv)

    for k in FAR_FIRST:
        expert_f(k).wait_recv()
    keep_f.wait()
    unpack(recv_f, rows_v)

    def hidden_f(u, carry):
        j, cols = unit_of(u)
        a = dot(rows_v[...], wg[j, :, cols])
        b = dot(rows_v[...], wu[j, :, cols])
        act_a[:, act_of(u)] = (a * jax.nn.sigmoid(a) * b).astype(BF16)
        return carry

    lax.fori_loop(0, 4, hidden_f, 0)

    def column_f(n):
        cols = pl.ds(pl.multiple_of(n * BLOCK, BLOCK), BLOCK)
        total = jnp.zeros((ROWS, BLOCK), F32)
        for j in range(2):
            total += dot(act_a[:, j * UNIT : (j + 1) * UNIT], wd[j, :, cols])
        return total

    emit_all(column_f, ret_f, got_f, tf_send, tf_recv)

    def hop(c, h, wide, src, dst, section, send_sem, recv_sem):
        cols = pl.ds(h * HALF + 2 * BLOCK * c, wide)
        return pltpu.make_async_remote_copy(
            src_ref=src.at[:, cols],
            dst_ref=dst.at[:, cols],
            send_sem=send_sem.at[2 * c + h],
            recv_sem=recv_sem.at[2 * c + h],
            device_id=(section, me),
            device_id_type=MESH,
        )

    def hops(src, dst, section, send_sem, recv_sem):
        return [
            hop(c, h, 2 * BLOCK if c < CHUNKS - 1 else BLOCK, src, dst, section, send_sem, recv_sem)
            for c in range(CHUNKS)
            for h in range(2)
        ]

    def combine(got, recv_sem, kinds, base, total, moves):
        for c in range(CHUNKS):
            wide = 2 * BLOCK if c < CHUNKS - 1 else BLOCK
            here = got.at[c, :, :, pl.ds(0, wide + LANES)]
            pltpu.make_async_copy(here, here, recv_sem.at[c]).wait()
            pieces = wide // LANES
            rows = got[c, :, :, :wide].reshape(MSG, wide)
            tail = got[c, :, :, wide : wide + LANES].reshape(MSG, LANES)
            main = sum(dot(hot_m[i], rows) for i in kinds)
            rest = sum(dot(hot_r[i, : 2 * pieces * TOK], tail) for i in kinds)
            for h in range(2):
                for i in range(pieces):
                    at = h * HALF + 2 * BLOCK * c + i * LANES
                    k = h * pieces + i
                    total[:, at : at + LANES] = (
                        base[:, at : at + LANES].astype(F32)
                        + main[h * TOK : (h + 1) * TOK, i * LANES : (i + 1) * LANES]
                        + rest[k * TOK : (k + 1) * TOK]
                    ).astype(BF16)
                moves[2 * c + h].start()

    moves_b = hops(sum_b, out_b, below, hb_send, hb_recv)
    moves_f = hops(sum_f, out_f, above, hf_send, hf_recv)
    for copy in bases:
        copy.wait()
    combine(got_b, tb_recv, (0,), base_c, sum_b, moves_b)
    combine(got_f, tf_recv, (1, 2), base_x, sum_f, moves_f)

    for k in FAR_FIRST:
        expert_v(k).wait_send()
        expert_f(k).wait_send()
    for copy in exchange:
        copy.wait_send()
    for ret, send_sem in ((ret_b, tb_send), (ret_f, tf_send)):
        for c in range(CHUNKS):
            wide = 2 * BLOCK if c < CHUNKS - 1 else BLOCK
            sent = ret.at[c, pl.ds(0, CHIPS - 1), :, pl.ds(0, wide + LANES)]
            pltpu.make_async_copy(sent, sent, send_sem.at[c]).wait()
    for copy in moves_b + moves_f:
        copy.wait()


def write_out(f, b, out_f, out_b, held, in_sem, out_sem):
    half = TOK // 2
    parts = [(i, pl.ds(j * half, half)) for i in range(2) for j in range(2)]
    loads = [
        pltpu.make_async_copy((f, b)[i].at[rows], held.at[i, rows], in_sem.at[n])
        for n, (i, rows) in enumerate(parts)
    ]
    stores = [
        pltpu.make_async_copy(held.at[i, rows], (out_f, out_b)[i].at[0, rows], out_sem.at[n])
        for n, (i, rows) in enumerate(parts)
    ]
    for load in loads:
        load.start()
    for load, store in zip(loads, stores):
        load.wait()
        store.start()
    for store in stores:
        store.wait()


def body(
    fwd_input, fwd_experts, fwd_gates, bwd_input, bwd_cotangent, bwd_experts, bwd_gates,
    w_gate, w_up, w_down,
):
    vmem, anywhere = pl.BlockSpec(memory_space=pltpu.VMEM), pl.BlockSpec(memory_space=pl.ANY)
    token_rows = jax.ShapeDtypeStruct((TOK, D), BF16)
    rows = pltpu.VMEM((TOK, D), BF16)
    messages = pltpu.VMEM((CHIPS, 16, WIDE), BF16)
    chunks = pltpu.VMEM((CHUNKS, CHIPS, 16, CHUNK), BF16)
    dma = pltpu.SemaphoreType.DMA
    out_f, out_b = pl.pallas_call(
        kernel,
        out_shape=(token_rows, token_rows),
        in_specs=[vmem] * 4 + [anywhere] * 6,
        out_specs=(anywhere, anywhere),
        scratch_shapes=[
            pltpu.VMEM((3, 2 * TOK, HALF), BF16),
            pltpu.VMEM((3, PIECES * TOK, PIECE), BF16),
        ]
        + [messages] * 6
        + [chunks] * 4
        + [
            pltpu.VMEM((2, D, UNIT), BF16),
            pltpu.VMEM((2, D, UNIT), BF16),
            pltpu.VMEM((2, UNIT, D), BF16),
            pltpu.VMEM((ROWS, D), BF16),
            pltpu.VMEM((ROWS, D), BF16),
            pltpu.VMEM((ROWS, 2 * UNIT), BF16),
            pltpu.VMEM((ROWS, 2 * UNIT), BF16),
            rows, rows, rows, rows,
            pltpu.VMEM((3, 2 * TOK, MSG), BF16),
            pltpu.VMEM((3, 8 * TOK, MSG), BF16),
            dma((27,)), dma((2,)), dma((3,)), dma((3,)), dma((3,)), dma((3,)),
        ]
        + [dma((CHIPS,))] * 6
        + [dma((CHUNKS,))] * 4
        + [dma((2 * CHUNKS,))] * 4,
        compiler_params=pltpu.CompilerParams(
            collective_id=0, has_side_effects=True, vmem_limit_bytes=60 << 20
        ),
        name="relay_experts",
    )(
        fwd_experts[0].T, fwd_gates[0].T, bwd_experts[0].T, bwd_gates[0].T,
        fwd_input[0], bwd_input[0], bwd_cotangent[0], w_gate[0], w_up[0], w_down[0],
    )
    result = jax.ShapeDtypeStruct((1, TOK, D), BF16)
    return pl.pallas_call(
        write_out,
        out_shape=(result, result),
        in_specs=[anywhere] * 2,
        out_specs=(anywhere, anywhere),
        scratch_shapes=[pltpu.VMEM((2, TOK, D), BF16), dma((4,)), dma((4,))],
        compiler_params=pltpu.CompilerParams(vmem_limit_bytes=60 << 20),
        name="write_out",
    )(out_f, out_b)


def solution(mesh):
    tokens = P("pp", "ep", None)
    in_specs = (tokens,) * 7 + (P("pp", None, "ep"), P("pp", None, "ep"), tokens)
    return jax.shard_map(
        body, mesh=mesh, in_specs=in_specs, out_specs=(tokens, tokens), check_vma=False
    )
```

time: 108 us -> 86.9 us (0.80)
  the two profiles are of different devices: /device:TPU:2 before, /device:TPU:8 now
where the time goes in v2:
time: 86.9 us; the launch traced here: 86.7 us
  Pallas kernels  86.1 us (99%)
    pallas_call x1, Pallas kernels, body(): pl.pallas_call(kernel, out_shape=(token_rows, token_rows), in_specs=[vmem...  84 us
    pallas_call x1, Pallas kernels, body(): pl.pallas_call(write_out, out_shape=(result, result), in_specs=[anywhere]...  2.04 us

profile of v2, /device:TPU:8, one launch (start us, length us, event | category | flops | bytes accessed | tf_op | source)
XLA Modules:
  0.0 86.7 jit_solution(1797865147304831442)
XLA Ops:
  0.6 84.0 %relay_experts.1 = (bf16[64,3584]{1,0:T(8,128)(2,1)}, bf16[64,3584]{1,0:T(8,128)(2,1)}) custom-call(s32[2,64]{1,0:T(2,128)} %bitcast.24, f32[2,64]{1,0:T(2,128)} %bitcast.25, s32[2,64]{1,0:T(2,128)} %bitcast.26, f32[2,64]{1,0:T(2,128)} %bitcast.27, bf16[64,3584]{1,0:T(8,128)(2,1)} %bitcast.21, bf16[64,3584]{1,0:T(8,128)(2,1)} %bitcast.22, ...), custom_call_target="tpu_custom_call" | custom-call | tf_op jit(solution)/shard_map/relay_experts/pallas_call | solution.py:449
  84.7 2.0 %write_out.1 = (bf16[1,64,3584]{2,1,0:T(8,128)(2,1)}, bf16[1,64,3584]{2,1,0:T(8,128)(2,1)}) custom-call(bf16[64,3584]{1,0:T(8,128)(2,1)} %get-tuple-element.4.f, bf16[64,3584]{1,0:T(8,128)(2,1)} %get-tuple-element.5.b), custom_call_target="tpu_custom_call" | custom-call | tf_op jit(solution)/shard_map/write_out/pallas_call | solution.py:485

commit v3 on v2

v3 whole, which is shorter than its diff:
```python
import jax
import jax.numpy as jnp
from jax import lax
from jax.experimental import pallas as pl
from jax.experimental.pallas import tpu as pltpu
from jax.sharding import PartitionSpec as P

MESH = pl.DeviceIdType.MESH
F32 = jnp.float32
BF16 = jnp.bfloat16

D = 3584
UNIT = 512
TOK = 64
CHIPS = 16
SIDE = 4
ROWS = 160
HALF = D // 2
PIECE = 512
PIECES = D // PIECE
WIDE = HALF + PIECE
MSG = CHIPS * 16
BLOCK = 256
LANES = 128
CHUNKS = 4
CHUNK = 2 * BLOCK + LANES
JOINT = 4
JOINT_PIECE = D // JOINT
GROUPS_F = 2 + 8
GROUPS_B = GROUPS_F + 2 * JOINT
FAR_FIRST = (10, 9, 14, 11, 6, 5, 13, 15, 7, 8, 2, 4, 1, 12, 3)


def dot(a, b):
    return lax.dot_general(a, b, (((1,), (0,)), ((), ())), preferred_element_type=F32)


def dot_nt(a, b):
    return lax.dot_general(a, b, (((1,), (1,)), ((), ())), preferred_element_type=F32)


def iota(shape, dim):
    return lax.broadcasted_iota(jnp.int32, shape, dim)


def as_hot(mask):
    return jnp.where(mask, 1.0, 0.0).astype(BF16)


def routing(ids, groups):
    expert = iota((CHIPS, TOK), 0)
    first, second = ids[0:1, :] == expert, ids[1:2, :] == expert
    hits = jnp.where(first | second, 1.0, 0.0)
    before = as_hot(iota((TOK, TOK), 0) < iota((TOK, TOK), 1))
    keys = hits * (dot(hits.astype(BF16), before) + 1.0)
    hots = groups * TOK
    copies = as_hot((iota((TOK, hots), 1) & (TOK - 1)) == iota((TOK, hots), 0))
    wide = dot(keys.astype(BF16), copies).astype(BF16)
    key = dot(rows_of_expert(BF16), wide)
    slot = iota((MSG, hots), 0) & 15
    group = iota((MSG, hots), 1) >> 6
    first_slot = (group - 2) * 2
    if groups > GROUPS_F:
        joint = group - GROUPS_F
        joint = jnp.where(joint < JOINT, joint * 4, (joint - JOINT) * 4 + 2)
        first_slot = jnp.where(group < GROUPS_F, first_slot, joint)
    want_main = (slot - 8 * group).astype(F32)
    want_rest = (slot - first_slot).astype(F32)
    main = (want_main >= 0.0) & (want_main < 8.0) & (key == want_main + 1.0)
    rest = (want_rest >= 0.0) & (want_rest < 2.0) & (key == want_rest + 9.0)
    hot = as_hot(main | rest)
    return key[:, :TOK], hot, first, second


def rows_of_expert(dtype):
    row, expert = iota((MSG, CHIPS), 0), iota((MSG, CHIPS), 1)
    return jnp.where((row >> 4) == expert, 1.0, 0.0).astype(dtype)


def slot_gates(key, first, second, gates):
    per = jnp.where(first, gates[0:1, :], 0.0) + jnp.where(second, gates[1:2, :], 0.0)
    spread = lax.dot_general(
        rows_of_expert(F32),
        per,
        (((1,), (0,)), ((), ())),
        precision=lax.Precision.HIGHEST,
        preferred_element_type=F32,
    )
    slot = iota((MSG, TOK), 0)
    main = key == (slot & 7).astype(F32) + 1.0
    rest = key == (slot & 1).astype(F32) + 9.0
    return (
        jnp.sum(jnp.where(main, spread, 0.0), axis=1, keepdims=True),
        jnp.sum(jnp.where(rest, spread, 0.0), axis=1, keepdims=True),
    )


def place(u, v):
    return (((u >> 1) & 15) << 4) + ((u >> 5) << 1) + (u & 1) == v


def place_joint(u, v):
    return (((u >> 1) & 15) << 4) + ((u >> 6) << 2) + (((u >> 5) & 1) << 1) + (u & 1) == v


def kernel(
    fids_in, fgates_in, bids_in, bgates_in, xf, xb, cb, gate, up, down,
    out_f, out_b,
    fids, fgates, bids, bgates, half_x, piece_x, joint_x, send_v, send_s, send_f, recv_v, recv_s, recv_f, ret_b, ret_f, got_b, got_f,
    wg, wu, wd, rows_f, rows_v, rows_s, pre_a, pre_b, act_a, act_b,
    base_x, base_c, sum_f, sum_b, hot_m, hot_r,
    small_sem, in_sem, joint_sem, base_sem, w_sem, own_sem, wx_send, wx_recv,
    sv_sem, rv_sem, ss_sem, rs_sem, sf_sem, rf_sem,
    tb_send, tb_recv, tf_send, tf_recv, hb_send, hb_recv, hf_send, hf_recv, ready,
):
    z, me = lax.axis_index("pp"), lax.axis_index("ep")
    sections = lax.axis_size("pp")
    chip, core = me // 2, lax.rem(me, 2)
    above, below = lax.rem(z + 1, sections), lax.rem(z + sections - 1, sections)
    sibling = chip * 2 + 1 - core

    def peer(k):
        x = lax.rem(chip // SIDE + k // SIDE, SIDE)
        y = lax.rem(lax.rem(chip, SIDE) + k % SIDE, SIDE)
        return x * SIDE + y

    barrier = pltpu.get_barrier_semaphore()
    for k in FAR_FIRST:
        pl.semaphore_signal(
            barrier, inc=1, device_id=(z, peer(k) * 2 + core), device_id_type=MESH
        )
    for target in ((z, sibling), (below, me)):
        pl.semaphore_signal(barrier, inc=1, device_id=target, device_id_type=MESH)

    small = [
        pltpu.make_async_copy(src, dst, small_sem.at[i])
        for i, (src, dst) in enumerate(
            ((fids_in, fids), (fgates_in, fgates), (bids_in, bids), (bgates_in, bgates))
        )
    ]
    loads = []
    for i, src in enumerate((xf, xb, cb)):
        own = [
            pltpu.make_async_copy(
                src.at[:, pl.ds(h * HALF, HALF)],
                half_x.at[i, pl.ds(h * TOK, TOK)],
                in_sem.at[i * 2 + h],
            )
            for h in range(2)
        ]
        pieces, width, at = (
            (piece_x, PIECE, 2 * JOINT)
            if i == 0
            else (joint_x.at[i - 1], JOINT_PIECE, (i - 1) * JOINT)
        )
        for k in range(D // width):
            own.append(
                pltpu.make_async_copy(
                    src.at[:, pl.ds(k * width, width)],
                    pieces.at[pl.ds(k * TOK, TOK)],
                    joint_sem.at[at + k],
                )
            )
        loads.append(own)
    for copy in small[:1] + loads[0] + small[1:] + loads[1] + loads[2]:
        copy.start()

    weights = [
        pltpu.make_async_copy(src, dst.at[0], w_sem.at[i])
        for i, (src, dst) in enumerate(((gate, wg), (up, wu), (down, wd)))
    ]
    bases = [
        pltpu.make_async_copy(xf, base_x, base_sem.at[0]),
        pltpu.make_async_copy(cb, base_c, base_sem.at[1]),
    ]

    def fill(dst, at, rows):
        width = rows.shape[1]
        dst[:, :, at : at + width] = rows.astype(BF16).reshape(CHIPS, 16, width)

    def to_expert(k, src, dst, send_sem, recv_sem):
        q = peer(k)
        return pltpu.make_async_remote_copy(
            src_ref=src.at[q],
            dst_ref=dst.at[chip],
            send_sem=send_sem.at[k],
            recv_sem=recv_sem.at[k],
            device_id=(z, q * 2 + core),
            device_id_type=MESH,
        )

    def expert_v(k):
        return to_expert(k, send_v, recv_v, sv_sem, rv_sem)

    def expert_s(k):
        return to_expert(k, send_s, recv_s, ss_sem, rs_sem)

    def expert_f(k):
        return to_expert(k, send_f, recv_f, sf_sem, rf_sem)

    keep_v, keep_s, keep_f = (
        pltpu.make_async_copy(src.at[chip], dst.at[chip], own_sem.at[i])
        for i, (src, dst) in enumerate(((send_v, recv_v), (send_s, recv_s), (send_f, recv_f)))
    )

    small[0].wait()
    key_f, hot_f, first_f, second_f = routing(fids[...], GROUPS_F)
    for copy in loads[0]:
        copy.wait()
    fill(send_f, 0, dot(hot_f[:, : 2 * TOK], half_x[0]))
    fill(send_f, HALF, dot(hot_f[:, 2 * TOK : 2 * TOK + PIECES * TOK], piece_x[...]))
    pl.semaphore_wait(barrier, CHIPS - 1 + 2)
    for k in FAR_FIRST:
        expert_f(k).start()
    keep_f.start()

    exchange = [
        pltpu.make_async_remote_copy(
            src_ref=src,
            dst_ref=dst.at[1],
            send_sem=wx_send.at[i],
            recv_sem=wx_recv.at[i],
            device_id=(z, sibling),
            device_id_type=MESH,
        )
        for i, (src, dst) in enumerate(((gate, wg), (up, wu), (down, wd)))
    ]
    for copy in weights + exchange + bases:
        copy.start()

    pl.semaphore_signal(ready, inc=1, device_id=(above, me), device_id_type=MESH)
    for copy in small[1:] + loads[1] + loads[2]:
        copy.wait()
    key_b, hot_b, first_b, second_b = routing(bids[...], GROUPS_B)
    scale_m, scale_r = slot_gates(key_b, first_b, second_b, bgates[...])
    joint_v = hot_b[:, GROUPS_F * TOK : (GROUPS_F + JOINT) * TOK]
    joint_s = hot_b[:, (GROUPS_F + JOINT) * TOK :]
    fill(send_v, 0, dot(hot_b[:, : 2 * TOK], half_x[1]))
    fill(send_v, HALF, dot(joint_v, joint_x[0]) + dot(joint_s, joint_x[1]) * scale_r)
    for k in FAR_FIRST:
        expert_f(k).wait_send()
        expert_v(k).start()
    keep_v.start()
    fill(send_s, 0, dot(hot_b[:, : 2 * TOK], half_x[2]) * scale_m)

    def flip(hot):
        n = hot.shape[1]
        unit = as_hot(iota((n, n), 0) == iota((n, n), 1))
        return dot_nt(unit, hot).astype(BF16)

    hot_m[0] = flip(hot_b[:, : 2 * TOK])
    hot_r[0] = flip(hot_b[:, 2 * TOK : GROUPS_F * TOK])
    scale_m, scale_r = slot_gates(key_f, first_f, second_f, fgates[...])
    high_m, high_r = scale_m.astype(BF16).astype(F32), scale_r.astype(BF16).astype(F32)
    hot_main, hot_rest = hot_f[:, : 2 * TOK].astype(F32), hot_f[:, 2 * TOK :].astype(F32)
    hot_m[1] = flip((hot_main * high_m).astype(BF16))
    hot_r[1] = flip((hot_rest * high_r).astype(BF16))
    hot_m[2] = flip((hot_main * (scale_m - high_m)).astype(BF16))
    hot_r[2] = flip((hot_rest * (scale_r - high_r)).astype(BF16))
    for k in FAR_FIRST:
        expert_v(k).wait_send()
        expert_s(k).start()
    keep_s.start()

    def unpack(src, dst):
        def step(i, carry):
            pair = src[pl.ds(2 * i, 2), :, :HALF].astype(F32)
            halves = pair.reshape(2, 2, 8, HALF)
            rows = pl.ds(pl.multiple_of(16 * i, 16), 16)
            dst[rows, :HALF] = halves[:, 0].reshape(16, HALF).astype(BF16)
            dst[rows, HALF:] = halves[:, 1].reshape(16, HALF).astype(BF16)
            return carry

        lax.fori_loop(0, CHIPS // 2, step, 0)

    def unit_of(u):
        return u // 2, pl.ds(pl.multiple_of(lax.rem(u, 2) * BLOCK, BLOCK), BLOCK)

    def act_of(u):
        return pl.ds(pl.multiple_of(u * BLOCK, BLOCK), BLOCK)

    def to_token(k, c, width, src, dst, send_sem, recv_sem):
        q = peer(k)
        return pltpu.make_async_remote_copy(
            src_ref=src.at[c, q, :, pl.ds(0, width)],
            dst_ref=dst.at[c, chip, :, pl.ds(0, width)],
            send_sem=send_sem.at[c],
            recv_sem=recv_sem.at[c],
            device_id=(z, q * 2 + core),
            device_id_type=MESH,
        )

    def emit(column, c, steps, ret):
        lows = [column(2 * c + i) for i in range(steps)]
        highs = [column(2 * c + i + 7) for i in range(steps)]
        for i in range(steps):
            main = jnp.concatenate(
                [y[:128].reshape(CHIPS, 8, BLOCK) for y in (lows[i], highs[i])], axis=1
            )
            ret[c, :, :, i * BLOCK : (i + 1) * BLOCK] = main.astype(BF16)
        rests = [
            y[128:, j * LANES : (j + 1) * LANES] for y in lows + highs for j in range(BLOCK // LANES)
        ]
        n = len(rests) * 32
        order = as_hot(place(iota((MSG, n), 1), iota((MSG, n), 0)))
        rest = dot(order, jnp.concatenate(rests, axis=0).astype(BF16))
        wide = steps * BLOCK
        ret[c, :, :, wide : wide + LANES] = rest.astype(BF16).reshape(CHIPS, 16, LANES)

    def keep(c, wide, ret, got, recv_sem):
        return pltpu.make_async_copy(
            ret.at[c, chip, :, pl.ds(0, wide + LANES)],
            got.at[c, chip, :, pl.ds(0, wide + LANES)],
            recv_sem.at[c],
        )

    widths = (2 * BLOCK,) * (CHUNKS - 1) + (BLOCK,)

    def hidden_ab(u, carry):
        j, cols = unit_of(u)
        pre_a[u] = dot(rows_v[...], wg[j, :, cols])
        pre_b[u] = dot(rows_v[...], wu[j, :, cols])
        return carry

    def hidden_f(u, carry):
        j, cols = unit_of(u)
        a = dot(rows_f[...], wg[j, :, cols])
        b = dot(rows_f[...], wu[j, :, cols])
        act_a[:, act_of(u)] = (a * jax.nn.sigmoid(a) * b).astype(BF16)
        return carry

    def hidden_b(u, carry):
        j, cols = unit_of(u)
        a, b = pre_a[u], pre_b[u]
        dh = dot_nt(rows_s[...], wd[j, cols, :])
        sig = jax.nn.sigmoid(a)
        act_a[:, act_of(u)] = (dh * b * sig * (1.0 + a * (1.0 - sig))).astype(BF16)
        act_b[:, act_of(u)] = (dh * (a * sig)).astype(BF16)
        return carry

    def column_f(n):
        cols = pl.ds(pl.multiple_of(n * BLOCK, BLOCK), BLOCK)
        total = jnp.zeros((ROWS, BLOCK), F32)
        for j in range(2):
            total += dot(act_a[:, j * UNIT : (j + 1) * UNIT], wd[j, :, cols])
        return total

    def column_b(n):
        rows = pl.ds(pl.multiple_of(n * BLOCK, BLOCK), BLOCK)
        total = jnp.zeros((ROWS, BLOCK), F32)
        for j in range(2):
            total += dot_nt(act_a[:, j * UNIT : (j + 1) * UNIT], wg[j, rows, :])
            total += dot_nt(act_b[:, j * UNIT : (j + 1) * UNIT], wu[j, rows, :])
        return total

    for k in FAR_FIRST:
        expert_f(k).wait_recv()
    keep_f.wait()
    unpack(recv_f, rows_f)
    n = PIECES * 32
    order = as_hot(place(iota((n, MSG), 0), iota((n, MSG), 1)))
    plain = dot(order, recv_f[:, :, HALF:].reshape(MSG, PIECE)).astype(BF16)
    for k in range(PIECES):
        rows_f[128:ROWS, k * PIECE : (k + 1) * PIECE] = plain[32 * k : 32 * k + 32]
    for copy in weights:
        copy.wait()
    lax.fori_loop(0, 2, hidden_f, 0)
    for copy in exchange:
        copy.wait_recv()
    lax.fori_loop(2, 4, hidden_f, 0)

    def step_f(c, carry):
        emit(column_f, c, 2, ret_f)
        return carry

    lax.fori_loop(0, CHUNKS - 1, step_f, 0)
    emit(column_f, CHUNKS - 1, 1, ret_f)

    for k in FAR_FIRST:
        expert_v(k).wait_recv()
    keep_v.wait()
    unpack(recv_v, rows_v)
    order = as_hot(place_joint(iota((MSG, MSG), 0), iota((MSG, MSG), 1)))
    plain = dot(order, recv_v[:, :, HALF:].reshape(MSG, JOINT_PIECE)).astype(BF16)
    for k in range(JOINT):
        cols = slice(k * JOINT_PIECE, (k + 1) * JOINT_PIECE)
        rows_v[128:ROWS, cols] = plain[64 * k : 64 * k + 32]
        rows_s[128:ROWS, cols] = plain[64 * k + 32 : 64 * k + 64]
    lax.fori_loop(0, 4, hidden_ab, 0)
    for k in FAR_FIRST:
        expert_s(k).wait_send()
        for c, wide in enumerate(widths):
            to_token(k, c, wide + LANES, ret_f, got_f, tf_send, tf_recv).start()
    for c, wide in enumerate(widths):
        keep(c, wide, ret_f, got_f, tf_recv).start()
    for k in FAR_FIRST:
        expert_s(k).wait_recv()
    keep_s.wait()
    unpack(recv_s, rows_s)
    lax.fori_loop(0, 4, hidden_b, 0)

    def send_back(c, wide):
        for k in FAR_FIRST:
            to_token(k, c, wide + LANES, ret_b, got_b, tb_send, tb_recv).start()
        keep(c, wide, ret_b, got_b, tb_recv).start()

    def step_b(c, carry):
        emit(column_b, c, 2, ret_b)
        send_back(c, 2 * BLOCK)
        return carry

    lax.fori_loop(0, CHUNKS - 1, step_b, 0)
    emit(column_b, CHUNKS - 1, 1, ret_b)
    send_back(CHUNKS - 1, BLOCK)

    def hop(c, h, wide, src, dst, section, send_sem, recv_sem):
        cols = pl.ds(h * HALF + 2 * BLOCK * c, wide)
        return pltpu.make_async_remote_copy(
            src_ref=src.at[:, cols],
            dst_ref=dst.at[:, cols],
            send_sem=send_sem.at[2 * c + h],
            recv_sem=recv_sem.at[2 * c + h],
            device_id=(section, me),
            device_id_type=MESH,
        )

    def hops(src, dst, section, send_sem, recv_sem):
        return [
            hop(c, h, 2 * BLOCK if c < CHUNKS - 1 else BLOCK, src, dst, section, send_sem, recv_sem)
            for c in range(CHUNKS)
            for h in range(2)
        ]

    def combine(got, recv_sem, kinds, base, total, moves):
        for c in range(CHUNKS):
            wide = 2 * BLOCK if c < CHUNKS - 1 else BLOCK
            here = got.at[c, :, :, pl.ds(0, wide + LANES)]
            pltpu.make_async_copy(here, here, recv_sem.at[c]).wait()
            pieces = wide // LANES
            rows = got[c, :, :, :wide].reshape(MSG, wide)
            tail = got[c, :, :, wide : wide + LANES].reshape(MSG, LANES)
            main = sum(dot(hot_m[i], rows) for i in kinds)
            rest = sum(dot(hot_r[i, : 2 * pieces * TOK], tail) for i in kinds)
            for h in range(2):
                for i in range(pieces):
                    at = h * HALF + 2 * BLOCK * c + i * LANES
                    k = h * pieces + i
                    total[:, at : at + LANES] = (
                        base[:, at : at + LANES].astype(F32)
                        + main[h * TOK : (h + 1) * TOK, i * LANES : (i + 1) * LANES]
                        + rest[k * TOK : (k + 1) * TOK]
                    ).astype(BF16)
                moves[2 * c + h].start()

    moves_b = hops(sum_b, out_b, below, hb_send, hb_recv)
    moves_f = hops(sum_f, out_f, above, hf_send, hf_recv)
    for copy in bases:
        copy.wait()
    combine(got_f, tf_recv, (1, 2), base_x, sum_f, moves_f)
    pl.semaphore_wait(ready, 1)
    combine(got_b, tb_recv, (0,), base_c, sum_b, moves_b)

    for copy in exchange:
        copy.wait_send()
    for ret, send_sem in ((ret_b, tb_send), (ret_f, tf_send)):
        for c in range(CHUNKS):
            wide = 2 * BLOCK if c < CHUNKS - 1 else BLOCK
            sent = ret.at[c, pl.ds(0, CHIPS - 1), :, pl.ds(0, wide + LANES)]
            pltpu.make_async_copy(sent, sent, send_sem.at[c]).wait()
    for copy in moves_b + moves_f:
        copy.wait()


def body(
    fwd_input, fwd_experts, fwd_gates, bwd_input, bwd_cotangent, bwd_experts, bwd_gates,
    w_gate, w_up, w_down,
):
    vmem, anywhere = pl.BlockSpec(memory_space=pltpu.VMEM), pl.BlockSpec(memory_space=pl.ANY)
    rows = pltpu.VMEM((TOK, D), BF16)
    messages = pltpu.VMEM((CHIPS, 16, WIDE), BF16)
    joint = pltpu.VMEM((CHIPS, 16, HALF + JOINT_PIECE), BF16)
    halves = pltpu.VMEM((CHIPS, 16, HALF), BF16)
    chunks = pltpu.VMEM((CHUNKS, CHIPS, 16, CHUNK), BF16)
    dma = pltpu.SemaphoreType.DMA
    out_f, out_b = pl.pallas_call(
        kernel,
        out_shape=(rows, rows),
        in_specs=[anywhere] * 10,
        out_specs=(vmem, vmem),
        scratch_shapes=[
            pltpu.VMEM((2, TOK), jnp.int32),
            pltpu.VMEM((2, TOK), F32),
            pltpu.VMEM((2, TOK), jnp.int32),
            pltpu.VMEM((2, TOK), F32),
            pltpu.VMEM((3, 2 * TOK, HALF), BF16),
            pltpu.VMEM((PIECES * TOK, PIECE), BF16),
            pltpu.VMEM((2, JOINT * TOK, JOINT_PIECE), BF16),
        ]
        + [joint, halves, messages] * 2
        + [chunks] * 4
        + [
            pltpu.VMEM((2, D, UNIT), BF16),
            pltpu.VMEM((2, D, UNIT), BF16),
            pltpu.VMEM((2, UNIT, D), BF16),
            pltpu.VMEM((ROWS, D), BF16),
            pltpu.VMEM((ROWS, D), BF16),
            pltpu.VMEM((ROWS, D), BF16),
            pltpu.VMEM((4, ROWS, BLOCK), F32),
            pltpu.VMEM((4, ROWS, BLOCK), F32),
            pltpu.VMEM((ROWS, 2 * UNIT), BF16),
            pltpu.VMEM((ROWS, 2 * UNIT), BF16),
            rows, rows, rows, rows,
            pltpu.VMEM((3, 2 * TOK, MSG), BF16),
            pltpu.VMEM((3, 8 * TOK, MSG), BF16),
            dma((4,)), dma((6,)), dma((2 * JOINT + PIECES,)), dma((2,)), dma((3,)), dma((3,)), dma((3,)), dma((3,)),
        ]
        + [dma((CHIPS,))] * 6
        + [dma((CHUNKS,))] * 4
        + [dma((2 * CHUNKS,))] * 4
        + [pltpu.SemaphoreType.REGULAR],
        compiler_params=pltpu.CompilerParams(
            collective_id=0, has_side_effects=True, vmem_limit_bytes=60 << 20
        ),
        name="relay_experts",
    )(
        fwd_experts[0].T, fwd_gates[0].T, bwd_experts[0].T, bwd_gates[0].T,
        fwd_input[0], bwd_input[0], bwd_cotangent[0], w_gate[0], w_up[0], w_down[0],
    )
    return out_f[None], out_b[None]


def solution(mesh):
    tokens = P("pp", "ep", None)
    in_specs = (tokens,) * 7 + (P("pp", None, "ep"), P("pp", None, "ep"), tokens)
    return jax.shard_map(
        body, mesh=mesh, in_specs=in_specs, out_specs=(tokens, tokens), check_vma=False
    )
```

time: 86.9 us -> 82.7 us (0.952)
  the two profiles are of different devices: /device:TPU:8 before, /device:TPU:96 now
where the time goes in v3:
time: 82.7 us; the launch traced here: 82.6 us
  Pallas kernels  80.4 us (97%)
  local copies, waits for them, and re-layouts  1.54 us (2%)
    pallas_call x1, Pallas kernels, body(): pl.pallas_call(kernel, out_shape=(rows, rows), in_specs=[anywhere] * 10,...  80.4 us

profile of v3, /device:TPU:96, one launch (start us, length us, event | category | flops | bytes accessed | tf_op | source)
XLA Modules:
  0.0 82.6 jit_solution(15832513929134963039)
XLA Ops:
  0.6 80.4 %relay_experts.1 = (bf16[64,3584]{1,0:T(8,128)(2,1)S(1)}, bf16[64,3584]{1,0:T(8,128)(2,1)S(1)}) custom-call(s32[2,64]{1,0:T(2,128)} %bitcast.28, f32[2,64]{1,0:T(2,128)} %bitcast.29, s32[2,64]{1,0:T(2,128)} %bitcast.30, f32[2,64]{1,0:T(2,128)} %bitcast.31, bf16[64,3584]{1,0:T(8,128)(2,1)} %bitcast.25, bf16[64,3584]{1,0:T(8,128)(2,1)} %bitcast.26, ...), custom_call_target="tpu_custom_call" | custom-call | tf_op jit(solution)/shard_map/relay_experts/pallas_call | solution.py:485
  81.1 0.8 copy.14
  81.8 0.8 copy.15

commit v4 on v3

--- a/solution.py
+++ b/solution.py
@@ -23,6 +23,7 @@
 BLOCK = 256
 LANES = 128
 CHUNKS = 4
+EARLY = 2
 CHUNK = 2 * BLOCK + LANES
 JOINT = 4
 JOINT_PIECE = D // JOINT
@@ -105,7 +106,7 @@
 
 def kernel(
     fids_in, fgates_in, bids_in, bgates_in, xf, xb, cb, gate, up, down,
-    out_f, out_b,
+    out,
     fids, fgates, bids, bgates, half_x, piece_x, joint_x, send_v, send_s, send_f, recv_v, recv_s, recv_f, ret_b, ret_f, got_b, got_f,
     wg, wu, wd, rows_f, rows_v, rows_s, pre_a, pre_b, act_a, act_b,
     base_x, base_c, sum_f, sum_b, hot_m, hot_r,
@@ -117,20 +118,14 @@
     sections = lax.axis_size("pp")
     chip, core = me // 2, lax.rem(me, 2)
     above, below = lax.rem(z + 1, sections), lax.rem(z + sections - 1, sections)
+    last = sections - 1
+    upward = z <= sections // 2
     sibling = chip * 2 + 1 - core
 
     def peer(k):
         x = lax.rem(chip // SIDE + k // SIDE, SIDE)
         y = lax.rem(lax.rem(chip, SIDE) + k % SIDE, SIDE)
         return x * SIDE + y
-
-    barrier = pltpu.get_barrier_semaphore()
-    for k in FAR_FIRST:
-        pl.semaphore_signal(
-            barrier, inc=1, device_id=(z, peer(k) * 2 + core), device_id_type=MESH
-        )
-    for target in ((z, sibling), (below, me)):
-        pl.semaphore_signal(barrier, inc=1, device_id=target, device_id_type=MESH)
 
     small = [
         pltpu.make_async_copy(src, dst, small_sem.at[i])
@@ -162,7 +157,25 @@
                 )
             )
         loads.append(own)
-    for copy in small[:1] + loads[0] + small[1:] + loads[1] + loads[2]:
+    for copy in small[:1] + loads[0]:
+        copy.start()
+    barrier = pltpu.get_barrier_semaphore()
+    for k in FAR_FIRST:
+        pl.semaphore_signal(
+            barrier, inc=1, device_id=(z, peer(k) * 2 + core), device_id_type=MESH
+        )
+    pl.semaphore_signal(barrier, inc=1, device_id=(z, sibling), device_id_type=MESH)
+
+    @pl.when(z < last)
+    def _():
+        pl.semaphore_signal(barrier, inc=1, device_id=(above, me), device_id_type=MESH)
+
+    @pl.when(z == 0)
+    def _():
+        pl.semaphore_signal(barrier, inc=1, device_id=(below, me), device_id_type=MESH)
+
+
+    for copy in small[1:] + loads[1] + loads[2]:
         copy.start()
 
     weights = [
@@ -209,7 +222,8 @@
         copy.wait()
     fill(send_f, 0, dot(hot_f[:, : 2 * TOK], half_x[0]))
     fill(send_f, HALF, dot(hot_f[:, 2 * TOK : 2 * TOK + PIECES * TOK], piece_x[...]))
-    pl.semaphore_wait(barrier, CHIPS - 1 + 2)
+    pl.semaphore_wait(barrier, CHIPS + (z + last - 1) // last + z // last)
+
     for k in FAR_FIRST:
         expert_f(k).start()
     keep_f.start()
@@ -228,7 +242,14 @@
     for copy in weights + exchange + bases:
         copy.start()
 
-    pl.semaphore_signal(ready, inc=1, device_id=(above, me), device_id_type=MESH)
+    @pl.when(z > 0)
+    def _():
+        pl.semaphore_signal(ready.at[0], inc=1, device_id=(below, me), device_id_type=MESH)
+
+    @pl.when(z == last)
+    def _():
+        pl.semaphore_signal(ready.at[1], inc=1, device_id=(above, me), device_id_type=MESH)
+
     for copy in small[1:] + loads[1] + loads[2]:
         copy.wait()
     key_b, hot_b, first_b, second_b = routing(bids[...], GROUPS_B)
@@ -353,6 +374,9 @@
             total += dot_nt(act_b[:, j * UNIT : (j + 1) * UNIT], wu[j, rows, :])
         return total
 
+    def return_f(k, c):
+        return to_token(k, c, widths[c] + LANES, ret_f, got_f, tf_send, tf_recv)
+
     for k in FAR_FIRST:
         expert_f(k).wait_recv()
     keep_f.wait()
@@ -389,10 +413,18 @@
     lax.fori_loop(0, 4, hidden_ab, 0)
     for k in FAR_FIRST:
         expert_s(k).wait_send()
-        for c, wide in enumerate(widths):
-            to_token(k, c, wide + LANES, ret_f, got_f, tf_send, tf_recv).start()
-    for c, wide in enumerate(widths):
-        keep(c, wide, ret_f, got_f, tf_recv).start()
+        for c in range(EARLY):
+            return_f(k, c).start()
+    for c in range(EARLY):
+        keep(c, widths[c], ret_f, got_f, tf_recv).start()
+
+    def late_f():
+        for c in range(EARLY, CHUNKS):
+            for k in FAR_FIRST:
+                return_f(k, c).start()
+            keep(c, widths[c], ret_f, got_f, tf_recv).start()
+
+    pl.when(jnp.logical_not(upward))(late_f)
     for k in FAR_FIRST:
         expert_s(k).wait_recv()
     keep_s.wait()
@@ -412,6 +444,8 @@
     lax.fori_loop(0, CHUNKS - 1, step_b, 0)
     emit(column_b, CHUNKS - 1, 1, ret_b)
     send_back(CHUNKS - 1, BLOCK)
+
+    pl.when(upward)(late_f)
 
     def hop(c, h, wide, src, dst, section, send_sem, recv_sem):
         cols = pl.ds(h * HALF + 2 * BLOCK * c, wide)
@@ -431,8 +465,8 @@
             for h in range(2)
         ]
 
-    def combine(got, recv_sem, kinds, base, total, moves):
-        for c in range(CHUNKS):
+    def combine(got, recv_sem, kinds, base, total, moves, chunks):
+        for c in chunks:
             wide = 2 * BLOCK if c < CHUNKS - 1 else BLOCK
             here = got.at[c, :, :, pl.ds(0, wide + LANES)]
             pltpu.make_async_copy(here, here, recv_sem.at[c]).wait()
@@ -452,13 +486,26 @@
                     ).astype(BF16)
                 moves[2 * c + h].start()
 
-    moves_b = hops(sum_b, out_b, below, hb_send, hb_recv)
-    moves_f = hops(sum_f, out_f, above, hf_send, hf_recv)
+    moves_b = hops(sum_b, out.at[1], below, hb_send, hb_recv)
+    moves_f = hops(sum_f, out.at[0], above, hf_send, hf_recv)
     for copy in bases:
         copy.wait()
-    combine(got_f, tf_recv, (1, 2), base_x, sum_f, moves_f)
-    pl.semaphore_wait(ready, 1)
-    combine(got_b, tb_recv, (0,), base_c, sum_b, moves_b)
+
+    @pl.when(z < last)
+    def _():
+        pl.semaphore_wait(ready.at[0], 1)
+
+    @pl.when(z == 0)
+    def _():
+        pl.semaphore_wait(ready.at[1], 1)
+
+    def combine_f(chunks):
+        combine(got_f, tf_recv, (1, 2), base_x, sum_f, moves_f, chunks)
+
+    combine_f(range(EARLY))
+    pl.when(jnp.logical_not(upward))(lambda: combine_f(range(EARLY, CHUNKS)))
+    combine(got_b, tb_recv, (0,), base_c, sum_b, moves_b, range(CHUNKS))
+    pl.when(upward)(lambda: combine_f(range(EARLY, CHUNKS)))
 
     for copy in exchange:
         copy.wait_send()
@@ -482,11 +529,11 @@
     halves = pltpu.VMEM((CHIPS, 16, HALF), BF16)
     chunks = pltpu.VMEM((CHUNKS, CHIPS, 16, CHUNK), BF16)
     dma = pltpu.SemaphoreType.DMA
-    out_f, out_b = pl.pallas_call(
+    out = pl.pallas_call(
         kernel,
-        out_shape=(rows, rows),
+        out_shape=pltpu.VMEM((2, TOK, D), BF16),
         in_specs=[anywhere] * 10,
-        out_specs=(vmem, vmem),
+        out_specs=vmem,
         scratch_shapes=[
             pltpu.VMEM((2, TOK), jnp.int32),
             pltpu.VMEM((2, TOK), F32),
@@ -517,7 +564,7 @@
         + [dma((CHIPS,))] * 6
         + [dma((CHUNKS,))] * 4
         + [dma((2 * CHUNKS,))] * 4
-        + [pltpu.SemaphoreType.REGULAR],
+        + [pltpu.SemaphoreType.REGULAR((2,))],
         compiler_params=pltpu.CompilerParams(
             collective_id=0, has_side_effects=True, vmem_limit_bytes=60 << 20
         ),
@@ -526,7 +573,7 @@
         fwd_experts[0].T, fwd_gates[0].T, bwd_experts[0].T, bwd_gates[0].T,
         fwd_input[0], bwd_input[0], bwd_cotangent[0], w_gate[0], w_up[0], w_down[0],
     )
-    return out_f[None], out_b[None]
+    return out[0:1], out[1:2]
 
 
 def solution(mesh):

time: 82.7 us -> 79.9 us (0.966); the launches traced: 82.6 us -> 78.9 us
  Pallas kernels: 80.4 us -> 77.2 us
    pallas_call x1, Pallas kernels: 80.4 us -> 77.2 us  [body(): pl.pallas_call(kernel, out_shape=pltpu.VMEM((2, TOK, D), BF16), in_specs=...]
    unnamed x2 -> x0, local copies, waits for them, and re-layouts: 1.54 us -> none
    slice x0 -> x1, local copies, waits for them, and re-layouts: none -> 0.98 us  [body(): return (out[0:1], out[1:2])]
where the time goes in v4:
time: 79.9 us; the launch traced here: 78.9 us
  Pallas kernels  77.2 us (97%)
  local copies, waits for them, and re-layouts  0.98 us (1%)
    pallas_call x1, Pallas kernels, body(): pl.pallas_call(kernel, out_shape=pltpu.VMEM((2, TOK, D), BF16), in_specs=...  77.2 us

profile of v4, /device:TPU:96, one launch (start us, length us, event | category | flops | bytes accessed | tf_op | source)
XLA Modules:
  0.0 78.9 jit_solution(9595274176035180717)
XLA Ops:
  0.6 77.2 %relay_experts.1 = bf16[2,64,3584]{2,1,0:T(8,128)(2,1)S(1)} custom-call(s32[2,64]{1,0:T(2,128)} %bitcast.24, f32[2,64]{1,0:T(2,128)} %bitcast.25, s32[2,64]{1,0:T(2,128)} %bitcast.26, f32[2,64]{1,0:T(2,128)} %bitcast.27, bf16[64,3584]{1,0:T(8,128)(2,1)} %bitcast.21, bf16[64,3584]{1,0:T(8,128)(2,1)} %bitcast.22, bf16[64,3584]{1,0:T(8,128)(2,1)} %bitcast.23, ...), custom_call_target="tpu_custom_call" | custom-call | tf_op jit(solution)/shard_map/relay_experts/pallas_call | solution.py:532
  77.9 1.0 %fusion = (bf16[1,64,3584]{2,1,0:T(8,128)(2,1)}, bf16[1,64,3584]{2,1,0:T(8,128)(2,1)}) fusion(bf16[2,64,3584]{2,1,0:T(8,128)(2,1)S(1)} %relay_experts.1), kind=kLoop, calls=%fused_computation | loop fusion | bytes 1835008 | tf_op jit(solution)/shard_map/slice | solution.py:576

commit v5 on v4

--- a/solution.py
+++ b/solution.py
@@ -109,7 +109,7 @@
     out,
     fids, fgates, bids, bgates, half_x, piece_x, joint_x, send_v, send_s, send_f, recv_v, recv_s, recv_f, ret_b, ret_f, got_b, got_f,
     wg, wu, wd, rows_f, rows_v, rows_s, pre_a, pre_b, act_a, act_b,
-    base_x, base_c, sum_f, sum_b, hot_m, hot_r,
+    base_x, base_c, sum_f, sum_b, left_f, hot_m, hot_r,
     small_sem, in_sem, joint_sem, base_sem, w_sem, own_sem, wx_send, wx_recv,
     sv_sem, rv_sem, ss_sem, rs_sem, sf_sem, rf_sem,
     tb_send, tb_recv, tf_send, tf_recv, hb_send, hb_recv, hf_send, hf_recv, ready,
@@ -119,7 +119,7 @@
     chip, core = me // 2, lax.rem(me, 2)
     above, below = lax.rem(z + 1, sections), lax.rem(z + sections - 1, sections)
     last = sections - 1
-    upward = z <= sections // 2
+    upward = z < last
     sibling = chip * 2 + 1 - core
 
     def peer(k):
@@ -157,8 +157,6 @@
                 )
             )
         loads.append(own)
-    for copy in small[:1] + loads[0]:
-        copy.start()
     barrier = pltpu.get_barrier_semaphore()
     for k in FAR_FIRST:
         pl.semaphore_signal(
@@ -175,6 +173,8 @@
         pl.semaphore_signal(barrier, inc=1, device_id=(below, me), device_id_type=MESH)
 
 
+    for copy in small[:1] + loads[0]:
+        copy.start()
     for copy in small[1:] + loads[1] + loads[2]:
         copy.start()
 
@@ -311,7 +311,7 @@
             device_id_type=MESH,
         )
 
-    def emit(column, c, steps, ret):
+    def emit(column, c, steps, ret, hold=None, extra=None):
         lows = [column(2 * c + i) for i in range(steps)]
         highs = [column(2 * c + i + 7) for i in range(steps)]
         for i in range(steps):
@@ -322,16 +322,21 @@
         rests = [
             y[128:, j * LANES : (j + 1) * LANES] for y in lows + highs for j in range(BLOCK // LANES)
         ]
-        n = len(rests) * 32
+        stacked = jnp.concatenate(rests, axis=0).astype(BF16)
+        if hold is not None:
+            hold[...] = stacked
+        if extra is not None:
+            stacked = jnp.concatenate([stacked, extra[...]], axis=0)
+        n = stacked.shape[0]
         order = as_hot(place(iota((MSG, n), 1), iota((MSG, n), 0)))
-        rest = dot(order, jnp.concatenate(rests, axis=0).astype(BF16))
+        rest = dot(order, stacked)
         wide = steps * BLOCK
         ret[c, :, :, wide : wide + LANES] = rest.astype(BF16).reshape(CHIPS, 16, LANES)
 
-    def keep(c, wide, ret, got, recv_sem):
+    def keep(c, width, ret, got, recv_sem):
         return pltpu.make_async_copy(
-            ret.at[c, chip, :, pl.ds(0, wide + LANES)],
-            got.at[c, chip, :, pl.ds(0, wide + LANES)],
+            ret.at[c, chip, :, pl.ds(0, width)],
+            got.at[c, chip, :, pl.ds(0, width)],
             recv_sem.at[c],
         )
 
@@ -374,8 +379,11 @@
             total += dot_nt(act_b[:, j * UNIT : (j + 1) * UNIT], wu[j, rows, :])
         return total
 
-    def return_f(k, c):
-        return to_token(k, c, widths[c] + LANES, ret_f, got_f, tf_send, tf_recv)
+    def width_f(c, shared):
+        return widths[c] + (0 if shared and c == CHUNKS - 1 else LANES)
+
+    def return_f(k, c, shared):
+        return to_token(k, c, width_f(c, shared), ret_f, got_f, tf_send, tf_recv)
 
     for k in FAR_FIRST:
         expert_f(k).wait_recv()
@@ -398,7 +406,7 @@
         return carry
 
     lax.fori_loop(0, CHUNKS - 1, step_f, 0)
-    emit(column_f, CHUNKS - 1, 1, ret_f)
+    emit(column_f, CHUNKS - 1, 1, ret_f, hold=left_f)
 
     for k in FAR_FIRST:
         expert_v(k).wait_recv()
@@ -414,17 +422,17 @@
     for k in FAR_FIRST:
         expert_s(k).wait_send()
         for c in range(EARLY):
-            return_f(k, c).start()
+            return_f(k, c, False).start()
     for c in range(EARLY):
-        keep(c, widths[c], ret_f, got_f, tf_recv).start()
-
-    def late_f():
+        keep(c, width_f(c, False), ret_f, got_f, tf_recv).start()
+
+    def late_f(shared):
         for c in range(EARLY, CHUNKS):
             for k in FAR_FIRST:
-                return_f(k, c).start()
-            keep(c, widths[c], ret_f, got_f, tf_recv).start()
-
-    pl.when(jnp.logical_not(upward))(late_f)
+                return_f(k, c, shared).start()
+            keep(c, width_f(c, shared), ret_f, got_f, tf_recv).start()
+
+    pl.when(jnp.logical_not(upward))(lambda: late_f(False))
     for k in FAR_FIRST:
         expert_s(k).wait_recv()
     keep_s.wait()
@@ -434,7 +442,7 @@
     def send_back(c, wide):
         for k in FAR_FIRST:
             to_token(k, c, wide + LANES, ret_b, got_b, tb_send, tb_recv).start()
-        keep(c, wide, ret_b, got_b, tb_recv).start()
+        keep(c, wide + LANES, ret_b, got_b, tb_recv).start()
 
     def step_b(c, carry):
         emit(column_b, c, 2, ret_b)
@@ -442,10 +450,10 @@
         return carry
 
     lax.fori_loop(0, CHUNKS - 1, step_b, 0)
-    emit(column_b, CHUNKS - 1, 1, ret_b)
+    emit(column_b, CHUNKS - 1, 1, ret_b, extra=left_f)
     send_back(CHUNKS - 1, BLOCK)
 
-    pl.when(upward)(late_f)
+    pl.when(upward)(lambda: late_f(True))
 
     def hop(c, h, wide, src, dst, section, send_sem, recv_sem):
         cols = pl.ds(h * HALF + 2 * BLOCK * c, wide)
@@ -465,16 +473,18 @@
             for h in range(2)
         ]
 
-    def combine(got, recv_sem, kinds, base, total, moves, chunks):
+    def combine(got, recv_sem, kinds, base, total, moves, chunks, shared=None):
         for c in chunks:
             wide = 2 * BLOCK if c < CHUNKS - 1 else BLOCK
-            here = got.at[c, :, :, pl.ds(0, wide + LANES)]
+            elsewhere = shared is not None and c == CHUNKS - 1
+            here = got.at[c, :, :, pl.ds(0, wide if elsewhere else wide + LANES)]
             pltpu.make_async_copy(here, here, recv_sem.at[c]).wait()
             pieces = wide // LANES
             rows = got[c, :, :, :wide].reshape(MSG, wide)
-            tail = got[c, :, :, wide : wide + LANES].reshape(MSG, LANES)
+            tail = (shared if elsewhere else got)[c, :, :, wide : wide + LANES].reshape(MSG, LANES)
+            first = 2 * pieces * TOK if elsewhere else 0
             main = sum(dot(hot_m[i], rows) for i in kinds)
-            rest = sum(dot(hot_r[i, : 2 * pieces * TOK], tail) for i in kinds)
+            rest = sum(dot(hot_r[i, first : first + 2 * pieces * TOK], tail) for i in kinds)
             for h in range(2):
                 for i in range(pieces):
                     at = h * HALF + 2 * BLOCK * c + i * LANES
@@ -499,21 +509,29 @@
     def _():
         pl.semaphore_wait(ready.at[1], 1)
 
-    def combine_f(chunks):
-        combine(got_f, tf_recv, (1, 2), base_x, sum_f, moves_f, chunks)
+    def combine_f(chunks, shared=None):
+        combine(got_f, tf_recv, (1, 2), base_x, sum_f, moves_f, chunks, shared)
 
     combine_f(range(EARLY))
     pl.when(jnp.logical_not(upward))(lambda: combine_f(range(EARLY, CHUNKS)))
     combine(got_b, tb_recv, (0,), base_c, sum_b, moves_b, range(CHUNKS))
-    pl.when(upward)(lambda: combine_f(range(EARLY, CHUNKS)))
+    pl.when(upward)(lambda: combine_f(range(EARLY, CHUNKS), got_b))
 
     for copy in exchange:
         copy.wait_send()
-    for ret, send_sem in ((ret_b, tb_send), (ret_f, tf_send)):
-        for c in range(CHUNKS):
-            wide = 2 * BLOCK if c < CHUNKS - 1 else BLOCK
-            sent = ret.at[c, pl.ds(0, CHIPS - 1), :, pl.ds(0, wide + LANES)]
-            pltpu.make_async_copy(sent, sent, send_sem.at[c]).wait()
+
+    def sent(ret, send_sem, c, width):
+        part = ret.at[c, pl.ds(0, CHIPS - 1), :, pl.ds(0, width)]
+        pltpu.make_async_copy(part, part, send_sem.at[c]).wait()
+
+    for c in range(CHUNKS):
+        sent(ret_b, tb_send, c, widths[c] + LANES)
+    for c in range(CHUNKS - 1):
+        sent(ret_f, tf_send, c, width_f(c, False))
+    pl.when(upward)(lambda: sent(ret_f, tf_send, CHUNKS - 1, width_f(CHUNKS - 1, True)))
+    pl.when(jnp.logical_not(upward))(
+        lambda: sent(ret_f, tf_send, CHUNKS - 1, width_f(CHUNKS - 1, False))
+    )
     for copy in moves_b + moves_f:
         copy.wait()
 
@@ -557,6 +575,7 @@
             pltpu.VMEM((ROWS, 2 * UNIT), BF16),
             pltpu.VMEM((ROWS, 2 * UNIT), BF16),
             rows, rows, rows, rows,
+            pltpu.VMEM((4 * 32, LANES), BF16),
             pltpu.VMEM((3, 2 * TOK, MSG), BF16),
             pltpu.VMEM((3, 8 * TOK, MSG), BF16),
             dma((4,)), dma((6,)), dma((2 * JOINT + PIECES,)), dma((2,)), dma((3,)), dma((3,)), dma((3,)), dma((3,)),

time: 79.9 us -> 79.9 us (level)
  no operation moved by 1% of the time
where the time goes in v5:
time: 79.9 us; the launch traced here: 78.3 us
  Pallas kernels  76.7 us (96%)
  local copies, waits for them, and re-layouts  0.98 us (1%)
    pallas_call x1, Pallas kernels, body(): pl.pallas_call(kernel, out_shape=pltpu.VMEM((2, TOK, D), BF16), in_specs=...  76.7 us

profile of v5, /device:TPU:96, one launch (start us, length us, event | category | flops | bytes accessed | tf_op | source)
XLA Modules:
  0.0 78.3 jit_solution(5356170204847718006)
XLA Ops:
  0.6 76.7 %relay_experts.1 = bf16[2,64,3584]{2,1,0:T(8,128)(2,1)S(1)} custom-call(s32[2,64]{1,0:T(2,128)} %bitcast.24, f32[2,64]{1,0:T(2,128)} %bitcast.25, s32[2,64]{1,0:T(2,128)} %bitcast.26, f32[2,64]{1,0:T(2,128)} %bitcast.27, bf16[64,3584]{1,0:T(8,128)(2,1)} %bitcast.21, bf16[64,3584]{1,0:T(8,128)(2,1)} %bitcast.22, bf16[64,3584]{1,0:T(8,128)(2,1)} %bitcast.23, ...), custom_call_target="tpu_custom_call" | custom-call | tf_op jit(solution)/shard_map/relay_experts/pallas_call | solution.py:550
  77.3 1.0 %fusion = (bf16[1,64,3584]{2,1,0:T(8,128)(2,1)}, bf16[1,64,3584]{2,1,0:T(8,128)(2,1)}) fusion(bf16[2,64,3584]{2,1,0:T(8,128)(2,1)S(1)} %relay_experts.1), kind=kLoop, calls=%fused_computation | loop fusion | bytes 1835008 | tf_op jit(solution)/shard_map/slice | solution.py:595
